TPU v7x, 32 devices: a whole 2x2x4 slice. The times are simulated.
32 devices in a mesh: ang: 8 (over y, x, core), row: 4 (over z).
Axes of the slice: x: 2, y: 2, z: 4, core: 2. Of those that a mesh axis runs over, the one named last changes fastest.
Arguments:
- dual_field: bfloat16 [32, 8, 2048], P('ang', 'row'), may hold values from -2 to 3
- forward: bfloat16 [32, 8, 2048], P('ang', 'row'), may hold values from -2 to 3
- sinogram: bfloat16 [32, 8, 2048], P('ang', 'row'), may hold values from -2 to 3
- first_weight: bfloat16 [3, 3, 32, 3], replicated, may hold values from -1.25 to 1.25
- first_bias: float32 [32], replicated, may hold values from -3 to 3
- middle_weight: bfloat16 [3, 3, 32, 32], replicated, may hold values from -0.375 to 0.375
- middle_bias: float32 [32], replicated, may hold values from -3 to 3
- last_weight: bfloat16 [3, 3, 1, 32], replicated, may hold values from -0.1875 to 0.1875
- magnify: float32 [32], P('ang'), may hold values from 0.85 to 0.95
- detector_shift: float32 [32], P('ang'), may hold values from -8 to 8
- row_fraction: float32 [32], P('ang'), may hold values from 0 to 1
- offsets: int32 [8, 16], replicated, may hold values from 0 to 3, as said below
- slab_order: int32 [16], replicated, may hold values from 0 to 15, each once
Outputs:
- new_dual: bfloat16 [32, 8, 2048], P('ang', 'row')
- volume: float32 [64, 2048], P('row', 'ang')
Inputs may be any that keep to these rules, and one draw needn't show every extreme that they name: offsets[b, q] lies within 2 rows of q * 3 // 15. `slab_order`: each slab appears once.
All inputs are finite; a program needn't handle non-finite values.
Results may differ from a plain program's by a relative error of at most 0.0022.
The roundings to bfloat16 on the way count: a program that leaves them out, or rounds other values in their place, can miss the bound.
Values may be sent and summed in bfloat16 or wider, within the bound.
A program may use at most 64 MiB of HBM per device.

v0:
```python
import math

import jax
import jax.numpy as jnp
from jax import lax
from jax.sharding import PartitionSpec as P

SLAB_Z = 4
SLABS_DEV = 4


def extended(x, sides, width):
    for axis, dim in sides:
        count, length = (lax.axis_size(axis), x.shape[dim])
        up = [(i, (i + 1) % count) for i in range(count)]
        down = [(j, i) for i, j in up]
        last = lax.slice_in_dim(x, length - width, length, axis=dim)
        first = lax.slice_in_dim(x, 0, width, axis=dim)
        before = lax.ppermute(last, axis, up)
        after = lax.ppermute(first, axis, down)
        x = jnp.concatenate([before, x, after], axis=dim)
    return x


def ramp_block(start, width, size):
    row_ids = lax.iota(jnp.int32, size)[:, None]
    col_ids = start + lax.iota(jnp.int32, width)[None, :]
    offset_odd = jnp.abs(row_ids - col_ids) % 2 == 1
    distance = jnp.where(offset_odd, row_ids - col_ids, 1).astype(jnp.float32)
    kernel = jnp.where(
        row_ids == col_ids,
        0.25,
        jnp.where(offset_odd, -1.0 / (math.pi * math.pi * distance * distance), 0.0),
    )
    return kernel.astype(jnp.bfloat16)


def conv_taps(inputs, weights):
    length = inputs.shape[1] - 2
    result = None
    for col_tap in range(3):
        partial_value = None
        for ang_tap in range(3):
            product = jnp.einsum(
                "oc,cau->oau",
                weights[ang_tap, col_tap],
                inputs[:, ang_tap : ang_tap + length],
                preferred_element_type=jnp.float32,
            )
            partial_value = product if partial_value is None else partial_value + product
        if col_tap == 0:
            partial_value = jnp.concatenate(
                [jnp.zeros_like(partial_value[:, :, :1]), partial_value[:, :, :-1]], axis=2
            )
        elif col_tap == 2:
            partial_value = jnp.concatenate(
                [partial_value[:, :, 1:], jnp.zeros_like(partial_value[:, :, :1])], axis=2
            )
        result = partial_value if result is None else result + partial_value
    return result


def conv_layer(inputs, weights, biases):
    return jax.nn.silu(conv_taps(inputs, weights) + biases[:, None, None]).astype(jnp.bfloat16)


def wrap_rims(values):
    return extended(values, (("ang", 2),), 1)


def interpolate(filtered, magnify, detector_shift):
    columns = filtered.shape[2]
    centre = (columns - 1) / 2.0
    places = (
        (lax.iota(jnp.float32, columns)[None, :] - centre) * magnify[:, None]
        + centre
        + detector_shift[:, None]
    )
    floors = jnp.floor(places)
    weight = (places - floors)[:, None, :]
    low_index = jnp.broadcast_to(floors.astype(jnp.int32)[:, None, :], filtered.shape)
    left_vals = jnp.take_along_axis(filtered, low_index, axis=2)
    right_vals = jnp.take_along_axis(filtered, low_index + 1, axis=2)
    return ((1.0 - weight) * left_vals + weight * right_vals).astype(jnp.bfloat16)


def band_starts(slots, offset_row):
    slab_ids = lax.iota(jnp.int32, offset_row.shape[0])
    return jnp.sum(jnp.where(slots[:, None] == slab_ids[None, :], offset_row[None, :], 0), axis=1)


def per_device(
    dual_field,
    forward,
    sinogram,
    first_weight,
    first_bias,
    middle_weight,
    middle_bias,
    last_weight,
    magnify,
    detector_shift,
    row_fraction,
    offsets,
    slab_order,
):
    angles_dev, rows_dev, columns = dual_field.shape
    stacked = jnp.stack([dual_field, forward, sinogram], axis=0).transpose(2, 0, 1, 3)

    def first_rows_layer(row_data):
        return conv_layer(row_data, first_weight, first_bias)

    def middle_rows_layer(row_data):
        return conv_layer(row_data, middle_weight, middle_bias)

    def last_rows_layer(row_data):
        return conv_taps(row_data, last_weight)[0]

    first_act = lax.map(first_rows_layer, wrap_rims(stacked))
    second_act = lax.map(middle_rows_layer, wrap_rims(first_act))
    update = lax.map(last_rows_layer, wrap_rims(second_act))
    new_dual = (dual_field.astype(jnp.float32) + update.transpose(1, 0, 2)).astype(jnp.bfloat16)
    flattened = new_dual.reshape(angles_dev * rows_dev, columns)

    def filter_block(block_id):
        return jnp.dot(
            flattened, ramp_block(block_id * 256, 256, columns), preferred_element_type=jnp.float32
        )

    pieces = lax.map(filter_block, jnp.arange(columns // 256, dtype=jnp.int32))
    filtered = pieces.transpose(1, 0, 2).reshape(angles_dev, rows_dev, columns)
    projected = interpolate(filtered, magnify, detector_shift)
    block_id = lax.axis_index("ang")
    row_id = lax.axis_index("row")
    offset_row = lax.dynamic_slice_in_dim(offsets, block_id, 1, 0)[0]
    depth_pos = lax.iota(jnp.int32, SLAB_Z)
    own_slots = lax.dynamic_slice_in_dim(slab_order, row_id * SLABS_DEV, SLABS_DEV, 0)
    first_rows = (band_starts(own_slots, offset_row)[:, None] + depth_pos[None, :]).reshape(-1)
    keep_weight = (1.0 - row_fraction)[:, None, None]
    take_weight = row_fraction[:, None, None]
    row_piece = lax.all_gather(projected, "row", axis=1, tiled=True)
    piece_rows = lax.iota(jnp.int32, row_piece.shape[1])
    near_rows = (piece_rows[None, :] == first_rows[:, None]).astype(jnp.bfloat16)
    next_rows = (piece_rows[None, :] == first_rows[:, None] + 1).astype(jnp.bfloat16)
    lower_rows = jnp.einsum("kn,anx->akx", near_rows, row_piece, preferred_element_type=jnp.float32)
    upper_rows = jnp.einsum("kn,anx->akx", next_rows, row_piece, preferred_element_type=jnp.float32)
    summed = jnp.sum(keep_weight * lower_rows + take_weight * upper_rows, axis=0)
    combined = lax.psum_scatter(summed, "ang", scatter_dimension=1, tiled=True)
    volume = combined / math.sqrt(angles_dev * lax.axis_size("ang"))
    return (new_dual, volume)


def solution(mesh):
    return jax.shard_map(
        per_device,
        mesh=mesh,
        in_specs=(
            P("ang", "row", None),
            P("ang", "row", None),
            P("ang", "row", None),
            P(),
            P(),
            P(),
            P(),
            P(),
            P("ang"),
            P("ang"),
            P("ang"),
            P(),
            P(),
        ),
        out_specs=(P("ang", "row", None), P("row", "ang")),
        check_vma=False,
    )
```

profile of v0, /device:TPU:0, one launch (start us, length us, event | category | flops | bytes accessed | tf_op | source)
XLA Modules:
  0.0 478.3 jit_solution(8038971433761409161)
XLA Ops:
  8.7 2.9 collective-permute-start.1
  11.7 1.4 broadcast_subtract_fusion
  15.9 10.5 %while.42 = (s32[]{:T(128)}, bf16[2,32,4,2048]{3,1,2,0:T(8,128)(2,1)S(1)}, bf16[2,3,6,2048]{3,1,2,0:T(4,128)(2,1)S(1)}, bf16[3,3,32,3]{2,3,1,0:T(4,128)(2,1)}, f32[32]{0:T(128)}, /*index=5*/s32[]{:T(128)}) while((s32[]{:T(128)}, bf16[2,32,4,2048]{3,1,2,0:T(8,128)(2,1)S(1)}, bf16[2,3,6,2048]{3,1,2,0:T(4,128)(2,1)S(1)}, ...), condition=%wide.region_1.2_spmd, body=%wide.region_0.1_spmd.sunk | while | flops 17825792 | bytes 20301716 | solution.py:119
  26.6 2.6 collective-permute-start.3
  29.5 4.9 %collective-permute-done.2 = bf16[2,32,1,2048]{3,1,2,0:T(8,128)(2,1)S(1)} collective-permute-done((bf16[2,32,1,2048]{3,1,2,0:T(8,128)(2,1)S(1)}, bf16[2,32,1,2048]{3,1,2,0:T(8,128)(2,1)S(1)}, u32[]{:S(2)}, u32[]{:S(2)}) %collective-permute-start.2) | collective-permute-done | bytes 262176 | tf_op jit(solution)/shard_map/ppermute | solution.py:19
  34.4 1.4 pad_maximum_fusion.1
  35.8 7.6 %while.43 = (s32[]{:T(128)}, bf16[2,32,4,2048]{3,2,1,0:T(4,128)(2,1)S(1)}, bf16[2,32,6,2048]{3,1,2,0:T(8,128)(2,1)S(1)}, bf16[3,3,32,32]{3,2,1,0:T(8,128)(2,1)S(1)}, f32[32]{0:T(128)}, /*index=5*/s32[]{:T(128)}) while((s32[]{:T(128)}, bf16[2,32,4,2048]{3,2,1,0:T(4,128)(2,1)S(1)}, bf16[2,32,6,2048]{3,1,2,0:T(8,128)(2,1)S(1)}, ...), condition=%wide.region_3.4_spmd, body=%wide.region_2.3_spmd.sunk | while | flops 154664960 | bytes 26812520 | solution.py:120
  44.2 2.2 collective-permute-start.4
  47.0 10.9 %collective-permute-done.4 = bf16[2,32,1,2048]{3,2,1,0:T(2,128)(2,1)S(1)} collective-permute-done((bf16[2,32,1,2048]{3,2,1,0:T(2,128)(2,1)S(1)}, bf16[2,32,1,2048]{3,2,1,0:T(2,128)(2,1)S(1)}, u32[]{:S(2)}, u32[]{:S(2)}) %collective-permute-start.4) | collective-permute-done | bytes 262176 | tf_op jit(solution)/shard_map/ppermute | solution.py:19
  58.8 2.9 pad_maximum_fusion
  61.7 9.5 %while.44 = (s32[]{:T(128)}, f32[2,4,2048]{2,0,1:T(2,128)S(1)}, bf16[2,32,6,2048]{3,2,1,0:T(8,128)(2,1)S(1)}, bf16[3,3,1,32]{3,2,1,0:T(2,128)(2,1)S(1)}, s32[]{:T(128)}, /*index=5*/s32[]{:T(128)}) while((s32[]{:T(128)}, f32[2,4,2048]{2,0,1:T(2,128)S(1)}, bf16[2,32,6,2048]{3,2,1,0:T(8,128)(2,1)S(1)}, bf16[3,3,1,32]{3,2,1,0:T(2,128)(2,1)S(1)}, ...), condition=%wide.region_5.6_spmd, body=%wide.region_4.5_spmd.sunk | while | flops 4784130 | bytes 10392077 | solution.py:121
  71.9 26.0 %while.45 = (s32[]{:T(128)}, f32[8,8,256]{2,1,0:T(8,128)S(1)}, s32[8]{0:T(128)S(1)}, bf16[8,2048]{1,0:T(8,128)(2,1)S(1)}, s32[]{:T(128)}, /*index=5*/s32[1]{0:T(128)}) while((s32[]{:T(128)}, f32[8,8,256]{2,1,0:T(8,128)S(1)}, s32[8]{0:T(128)S(1)}, bf16[8,2048]{1,0:T(8,128)(2,1)S(1)}, s32[]{:T(128)}, /*index=5*/s32[1]{0:T(128)}) %tuple.107), condition=%wide.region_7.8_spmd, body=%wide.region_6.7_spmd.sunk | while | flops 20447492 | bytes 43109 | solution.py:130
  73.3 1.9 fusion.327
  76.6 1.9 fusion.327
  79.8 1.9 fusion.327
  83.1 1.9 fusion.327
  86.3 1.9 fusion.327
  89.6 1.9 fusion.327
  92.8 1.9 fusion.327
  96.1 1.9 fusion.327
  98.1 160.1 %gather_fusion = f32[16384]{0:T(1024)S(1)} fusion(f32[4,2,2048]{2,1,0:T(2,128)S(1)} %reshape.212, s32[16384]{0:T(1024)S(1)} %bitcast.415), kind=kCustom, calls=%fused_computation.clone | custom fusion | bytes 327680 | tf_op jit(solution)/shard_map/jit(take_along_axis)/gather | solution.py:82
  258.2 160.1 %gather_fusion.1 = f32[16384]{0:T(1024)S(1)} fusion(f32[4,2,2048]{2,1,0:T(2,128)S(1)} %reshape.212, s32[16384]{0:T(1024)S(1)} %bitcast.414), kind=kCustom, calls=%fused_computation.1.clone | custom fusion | bytes 327680 | tf_op jit(solution)/shard_map/jit(take_along_axis)/gather | solution.py:83
  418.6 16.0 %all_gather.3 = bf16[4,8,2048]{2,0,1:T(4,128)(2,1)S(1)} all-gather(bf16[4,2,2048]{2,0,1:T(4,128)(2,1)S(1)} %copy.56), channel_id=1, replica_groups=mesh['ang'=8,'row'=4] {'row'}, dimensions={1}, use_global_device_ids=true | all-gather | bytes 163840 | tf_op jit(solution)/shard_map/all_gather | solution.py:141
  435.9 34.2 %reduce-scatter.2.cloned.1.call-done = f32[16,256]{1,0:T(8,128)} async-done(((f32[16,2048]{1,0:T(8,128)}), f32[16,256]{1,0:T(8,128)}) %reduce-scatter.2.cloned.1.call-update) | async-done | bytes 16400 | tf_op jit(solution)/shard_map/reduce_scatter | solution.py:148
  (177 shorter events, 43.0 us)
Async XLA Ops:
  7.2 7.5 %copy-start = (s32[8,16]{1,0:T(8,128)S(1)}, s32[8,16]{1,0:T(8,128)}, u32[]{:S(2)}) copy-start(s32[8,16]{1,0:T(8,128)} %param.34) | copy-start | bytes 1540
  7.2 462.9 %reduce-scatter.2.cloned.1.call-start = ((), (), s32[]{:S(2)}) async-start(), calls=%async_computation.1 | async-start | bytes 147456 | tf_op jit(solution)/shard_map/reduce_scatter | solution.py:148
  8.2 7.4 %collective-permute-start = (bf16[2,3,1,2048]{3,0,2,1:T(2,128)(2,1)S(1)}, bf16[2,3,1,2048]{3,0,2,1:T(2,128)(2,1)S(1)}, u32[]{:S(2)}, u32[]{:S(2)}) collective-permute-start(bf16[2,3,1,2048]{3,0,2,1:T(2,128)(2,1)S(1)} %get-tuple-element.220), channel_id=1, source_target_pairs={{0,4},{4,8},{8,12},{12,16},{16,20},{20,24},{24,28},{28,0},{1,5},{5... | collective-permute-start | bytes 73736 | tf_op jit(solution)/shard_map/ppermute | solution.py:19
  8.7 6.9 %collective-permute-start.1 = (bf16[2,3,1,2048]{3,0,2,1:T(2,128)(2,1)S(1)}, bf16[2,3,1,2048]{3,0,2,1:T(2,128)(2,1)S(1)}, u32[]{:S(2)}, u32[]{:S(2)}) collective-permute-start(bf16[2,3,1,2048]{3,0,2,1:T(2,128)(2,1)S(1)} %get-tuple-element.221), channel_id=1, source_target_pairs={{4,0},{8,4},{12,8},{16,12},{20,16},{24,20},{28,24},{0,28},{5,1},{9... | collective-permute-start | bytes 73736 | tf_op jit(solution)/shard_map/ppermute | solution.py:20
  14.6 14.7 %copy-start.9 = (pred[4,2048]{1,0:T(4,128)(4,1)}, pred[4,2048]{1,0:T(4,128)(4,1)S(1)}, u32[]{:S(2)}) copy-start(pred[4,2048]{1,0:T(4,128)(4,1)S(1)} %get-tuple-element.229) | copy-start | bytes 24580
  16.0 2.1 copy-start.4
  19.9 0.7 copy-start.14
  21.2 2.1 copy-start.4
  25.1 0.7 copy-start.14
  26.5 2.8 copy-start.1
  26.5 9.3 %copy-start.2 = (bf16[3,3,32,32]{3,2,1,0:T(8,128)(2,1)S(1)}, bf16[3,3,32,32]{3,2,1,0:T(8,128)(2,1)}, u32[]{:S(2)}) copy-start(bf16[3,3,32,32]{3,2,1,0:T(8,128)(2,1)} %param.28) | copy-start | bytes 55300
  26.6 7.9 %collective-permute-start.2 = (bf16[2,32,1,2048]{3,1,2,0:T(8,128)(2,1)S(1)}, bf16[2,32,1,2048]{3,1,2,0:T(8,128)(2,1)S(1)}, u32[]{:S(2)}, u32[]{:S(2)}) collective-permute-start(bf16[2,32,1,2048]{3,1,2,0:T(8,128)(2,1)S(1)} %get-tuple-element.218), channel_id=1, source_target_pairs={{0,4},{4,8},{8,12},{12,16},{16,20},{20,24},{24,28},{28,0},{1,5},{5... | collective-permute-start | bytes 786440 | tf_op jit(solution)/shard_map/ppermute | solution.py:19
  26.6 7.8 %collective-permute-start.3 = (bf16[2,32,1,2048]{3,1,2,0:T(8,128)(2,1)S(1)}, bf16[2,32,1,2048]{3,1,2,0:T(8,128)(2,1)S(1)}, u32[]{:S(2)}, u32[]{:S(2)}) collective-permute-start(bf16[2,32,1,2048]{3,1,2,0:T(8,128)(2,1)S(1)} %get-tuple-element.219), channel_id=1, source_target_pairs={{4,0},{8,4},{12,8},{16,12},{20,16},{24,20},{28,24},{0,28},{5,1},{9... | collective-permute-start | bytes 786440 | tf_op jit(solution)/shard_map/ppermute | solution.py:20
  38.0 0.7 copy-start.15
  43.4 3.5 copy-start.13
  43.4 3.5 copy-start.12
  44.2 13.8 %collective-permute-start.4 = (bf16[2,32,1,2048]{3,2,1,0:T(2,128)(2,1)S(1)}, bf16[2,32,1,2048]{3,2,1,0:T(2,128)(2,1)S(1)}, u32[]{:S(2)}, u32[]{:S(2)}) collective-permute-start(bf16[2,32,1,2048]{3,2,1,0:T(2,128)(2,1)S(1)} %get-tuple-element.216), channel_id=1, source_target_pairs={{0,4},{4,8},{8,12},{12,16},{16,20},{20,24},{24,28},{28,0},{1,5},{5... | collective-permute-start | bytes 786440 | tf_op jit(solution)/shard_map/ppermute | solution.py:19
  46.4 12.4 %collective-permute-start.5 = (bf16[2,32,1,2048]{3,2,1,0:T(2,128)(2,1)S(1)}, bf16[2,32,1,2048]{3,2,1,0:T(2,128)(2,1)}, u32[]{:S(2)}, u32[]{:S(2)}) collective-permute-start(bf16[2,32,1,2048]{3,2,1,0:T(2,128)(2,1)S(1)} %get-tuple-element.217), channel_id=1, source_target_pairs={{4,0},{8,4},{12,8},{16,12},{20,16},{24,20},{28,24},{0,28},{5,1},{9... | collective-permute-start | bytes 786440 | tf_op jit(solution)/shard_map/ppermute | solution.py:20
  58.0 0.8 copy-start.3
  61.7 9.6 %copy-start.8 = (bf16[4,2,2048]{2,1,0:T(2,128)(2,1)S(1)}, bf16[4,2,2048]{2,1,0:T(2,128)(2,1)}, u32[]{:S(2)}) copy-start(bf16[4,2,2048]{2,1,0:T(2,128)(2,1)} %param.23) | copy-start | bytes 98308
  61.7 9.7 %copy-start.11 = (f32[8,8,256]{2,1,0:T(8,128)S(1)}, f32[8,8,256]{2,1,0:T(8,128)}, u32[]{:S(2)}) copy-start(f32[8,8,256]{2,1,0:T(8,128)} %custom-call.9) | copy-start | bytes 196612
  258.2 160.1 %copy-start.5 = (f32[4,2048]{1,0:T(4,128)S(1)}, f32[4,2048]{1,0:T(4,128)}, u32[]{:S(2)}) copy-start(f32[4,2048]{1,0:T(4,128)} %get-tuple-element.222) | copy-start | bytes 98308
  258.2 160.1 %copy-start.6 = (f32[4,2048]{1,0:T(4,128)S(1)}, f32[4,2048]{1,0:T(4,128)}, u32[]{:S(2)}) copy-start(f32[4,2048]{1,0:T(4,128)} %get-tuple-element.223) | copy-start | bytes 98308
  258.2 160.1 %copy-start.10 = (pred[4,2048]{1,0:T(4,128)(4,1)S(1)}, pred[4,2048]{1,0:T(4,128)(4,1)}, u32[]{:S(2)}) copy-start(pred[4,2048]{1,0:T(4,128)(4,1)} %copy-done.9) | copy-start | bytes 24580
  (2 other events, 1.3 us)
Sparse Core Ops, SparseCore 0:
  436.0 34.0 reduce-scatter.1
where the time goes:
time: 479 us; the launch traced here: 478 us
  local copies, waits for them, and re-layouts  333 us (70%)
  waiting for transfers between devices  50.1 us (10%)
  matrix products  38.5 us (8%)
  blocking collectives  16 us (3%)
  between operations  14.4 us (3%)
  other arithmetic  10.7 us (2%)
  starting transfers between devices  8.89 us (2%)
  loops' own time  6.17 us (1%)
    gather x2, local copies, waits for them, and re-layouts, interpolate(): right_vals = jnp.take_along_axis(filtered, low_index + 1, axis=2)  160 us
    gather x2, local copies, waits for them, and re-layouts, interpolate(): left_vals = jnp.take_along_axis(filtered, low_index, axis=2)  160 us
    reduce_scatter x1, waiting for transfers between devices, per_device(): combined = lax.psum_scatter(summed, 'ang', scatter_dimension=1, tiled=True)  34.2 us
    dot_general x54, matrix products, conv_taps(): jnp.einsum('oc,cau->oau', weights[ang_tap, col_tap], inputs[:, ang_tap:an...  22.2 us
    all_gather x1, blocking collectives, per_device(): row_piece = lax.all_gather(projected, 'row', axis=1, tiled=True)  16 us
    ppermute x3, waiting for transfers between devices, extended(): before = lax.ppermute(last, axis, up)  15.8 us
    dot_general x8, matrix products, filter_block(): jnp.dot(flattened, ramp_block(block_id * 256, 256, columns), preferred_el...  15 us
  transfers between devices with their start and end apart: 7, of which 3 were waited for; matrix products, arithmetic and copies ran while one was open for 1% of the time, Pallas kernels for 0%

commit v1 on v0

v1 whole, which is shorter than its diff:
```python
import functools
import math

import jax
import jax.numpy as jnp
from jax import lax
from jax.experimental import pallas as pl
from jax.experimental.pallas import tpu as pltpu
from jax.sharding import PartitionSpec as P

SLAB_Z = 4
MAG_LOW, MAG_HIGH, SHIFT_MAX = 0.85, 0.95, 8.0
PAD = 128
TILE = 256
F32 = jnp.float32
BF16 = jnp.bfloat16
MESH = pl.DeviceIdType.MESH


def dot(a, b):
    return jnp.dot(a, b, preferred_element_type=F32)


def silu(v):
    half = 0.5 * v
    return half + half * jnp.tanh(half)


def iota(shape, dim):
    return lax.broadcasted_iota(jnp.int32, shape, dim)


def as_column(row):
    size = row.shape[1]
    spread = jnp.broadcast_to(row, (size, size))
    return jnp.sum(
        jnp.where(iota((size, size), 0) == iota((size, size), 1), spread, 0.0), axis=1, keepdims=True
    )


def by_row(ref, shape, period):
    index = iota(shape, 0) // 2
    value = jnp.full(shape, ref[0], F32)
    for a in range(1, period):
        value = jnp.where(index == a, ref[a], value)
    return value


def shifted(window, width):
    size = window.shape[1]
    left = pltpu.roll(window, 1, 1)[:, PAD : PAD + width]
    right = pltpu.roll(window, size - 1, 1)[:, PAD : PAD + width]
    mid = window[:, PAD : PAD + width]
    return jnp.concatenate([left.astype(BF16), mid.astype(BF16), right.astype(BF16)], axis=0)


def kernel(
    n_ang, n_row, dual, forward, sino, fw, fb, mw, mb, lw, mag, shift, frac, offsets, order,
    nd_out, vol_out,
    halo, x1, x2, x3, taps, w1, w2, w3, ramp, frac_own, frac_all, sent, got,
    halo_send, halo_recv, frac_send, frac_recv, send_sem, recv_sem,
):
    angs, rows, cols = dual.shape
    ch = fw.shape[2]
    total = n_ang * n_row
    my_ang, my_row = lax.axis_index("ang"), lax.axis_index("row")
    me = my_ang * n_row + my_row
    wide = angs + 6
    out1, out2 = angs + 4, angs + 2
    ar = angs * rows
    per = 64

    def place_of(step):
        target = lax.rem(me + step, total)
        return target, target // n_row, lax.rem(target, n_row)

    barrier = pltpu.get_barrier_semaphore()

    def greet(step, carry):
        _, ang, row = place_of(step)
        pl.semaphore_signal(barrier, inc=1, device_id=(ang, row), device_id_type=MESH)
        return carry

    lax.fori_loop(1, total, greet, 0)

    lane = iota((8, 128), 1)
    mine = jnp.full((8, 128), frac[0], F32)
    for a in range(1, angs):
        mine = jnp.where((lane // rows) % angs == a, frac[a], mine)
    frac_own[...] = mine
    frac_all[my_ang] = mine
    pl.semaphore_wait(barrier, total - 1)

    left = lax.rem(my_ang + n_ang - 1, n_ang)
    right = lax.rem(my_ang + 1, n_ang)
    halo_copies = []
    for c, ref in enumerate((dual, forward, sino)):
        for side, (peer, first) in enumerate(((right, angs - 3), (left, 0))):
            copy = pltpu.make_async_remote_copy(
                src_ref=ref.at[pl.ds(first, 3)],
                dst_ref=halo.at[side, c],
                send_sem=halo_send.at[side, c],
                recv_sem=halo_recv.at[side, c],
                device_id=(peer, my_row),
                device_id_type=MESH,
            )
            copy.start()
            halo_copies.append(copy)

    def frac_copy(source, target):
        return pltpu.make_async_remote_copy(
            src_ref=frac_own,
            dst_ref=frac_all.at[source],
            send_sem=frac_send.at[target],
            recv_sem=frac_recv.at[source],
            device_id=(target, my_row),
            device_id_type=MESH,
        )

    def frac_start(step, carry):
        frac_copy(my_ang, lax.rem(my_ang + step, n_ang)).start()
        return carry

    lax.fori_loop(1, n_ang, frac_start, 0)

    k1 = 3 * per
    pick1 = iota((3, k1), 1) % per // (wide * rows) == iota((3, k1), 0)
    pick1 = jnp.where(pick1, 1.0, 0.0).astype(BF16)
    place1 = iota((ch, k1), 1)
    tap1, rest1 = place1 // per, place1 % per
    ang1 = jnp.where(rest1 < 3 * wide * rows, rest1 % (wide * rows) // rows, -9)
    row1 = rest1 % rows
    tiles1 = [[dot(fw[i, j], pick1) for j in range(3)] for i in range(3)]
    joined1 = [
        jnp.where(tap1 == 0, tiles1[i][0], jnp.where(tap1 == 1, tiles1[i][1], tiles1[i][2]))
        for i in range(3)
    ]
    for r in range(rows):
        for a in range(out1):
            block = jnp.zeros((ch, k1), F32)
            for i in range(3):
                block = jnp.where((ang1 == a + i) & (row1 == r), joined1[i], block)
            w1[pl.ds((r * out1 + a) * ch, ch), :] = block.astype(BF16)

    k2 = out1 * ch
    pick2 = jnp.where(iota((ch, k2), 1) % ch == iota((ch, k2), 0), 1.0, 0.0).astype(BF16)
    ang2 = iota((ch, k2), 1) // ch
    for j in range(3):
        tiles2 = [dot(mw[i, j], pick2) for i in range(3)]
        for a in range(out2):
            block = jnp.zeros((ch, k2), F32)
            for i in range(3):
                block = jnp.where(ang2 == a + i, tiles2[i], block)
            w2[pl.ds(a * ch, ch), pl.ds(j * k2, k2)] = block.astype(BF16)

    k3 = rows * out2 * ch
    pick3 = jnp.where(iota((ch, k3), 1) % ch == iota((ch, k3), 0), 1.0, 0.0).astype(BF16)
    place3 = iota((ar, k3), 1)
    ang3 = place3 // ch % out2 - iota((ar, k3), 0) // rows
    same3 = place3 // (out2 * ch) == iota((ar, k3), 0) % rows
    for j in range(3):
        block = jnp.zeros((ar, k3), F32)
        for i in range(3):
            weights = jnp.broadcast_to(lw[i, j].astype(F32), (ar, ch)).astype(BF16)
            block = jnp.where((ang3 == i) & same3, dot(weights, pick3), block)
        w3[pl.ds(j * ar, ar), :] = block

    blocks = cols // TILE

    def ramp_block(b, carry):
        away = (b - (blocks - 1)) * TILE + iota((TILE, TILE), 1) - iota((TILE, TILE), 0)
        odd = away % 2 == 1
        distance = jnp.where(odd, away, 1).astype(F32)
        value = jnp.where(odd, -1.0 / (math.pi * math.pi * distance * distance), 0.0)
        ramp[b] = jnp.where(away == 0, 0.25, value).astype(BF16)
        return carry

    lax.fori_loop(0, 2 * blocks - 1, ramp_block, 0)

    bias1 = jnp.concatenate([as_column(fb[...])] * (rows * out1), axis=0)
    bias2 = jnp.concatenate([as_column(mb[...])] * out2, axis=0)

    x1[...] = jnp.zeros_like(x1)
    x2[:, pl.ds(0, PAD)] = jnp.zeros((x2.shape[0], PAD), F32)
    x2[:, pl.ds(PAD + cols, PAD)] = jnp.zeros((x2.shape[0], PAD), F32)
    for c, ref in enumerate((dual, forward, sino)):
        for a in range(angs):
            x1[pl.ds((c * wide + 3 + a) * rows, rows), pl.ds(PAD, cols)] = ref[a].astype(F32)
    for copy in halo_copies:
        copy.wait()
    for c in range(3):
        for a in range(3):
            x1[pl.ds((c * wide + a) * rows, rows), pl.ds(PAD, cols)] = halo[0, c, a].astype(F32)
            x1[pl.ds((c * wide + 3 + angs + a) * rows, rows), pl.ds(PAD, cols)] = halo[1, c, a].astype(F32)

    def layer1(t, carry):
        start = pl.multiple_of(t * TILE, TILE)
        stack = shifted(x1[:, pl.ds(start, TILE + 2 * PAD)], TILE)
        x2[:, pl.ds(start + PAD, TILE)] = silu(dot(w1[...], stack) + bias1)
        return carry

    lax.fori_loop(0, blocks, layer1, 0)

    def layer2(t, carry):
        start = pl.multiple_of(t * TILE, TILE)
        for r in range(rows):
            stack = shifted(x2[pl.ds(r * k2, k2), pl.ds(start, TILE + 2 * PAD)], TILE)
            value = silu(dot(w2[...], stack) + bias2)
            x3[pl.ds(r * out2 * ch, out2 * ch), :] = value.astype(BF16)
        taps[:, pl.ds(start, TILE)] = dot(w3[...].astype(BF16), x3[...])
        return carry

    lax.fori_loop(0, blocks, layer2, 0)

    column = iota((ar, cols), 1)
    before = jnp.where(column == 0, 0.0, pltpu.roll(taps[0:ar, :], 1, 1))
    after = jnp.where(column == cols - 1, 0.0, pltpu.roll(taps[2 * ar : 3 * ar, :], cols - 1, 1))
    update = before + taps[ar : 2 * ar, :] + after
    own = x1[pl.ds(3 * rows, ar), pl.ds(PAD, cols)]
    new_dual = (own + update).astype(BF16).astype(F32)
    for a in range(angs):
        nd_out[a] = new_dual[a * rows : (a + 1) * rows].astype(BF16)

    pieces = jnp.concatenate(
        [new_dual[:, b * TILE : (b + 1) * TILE] for b in range(blocks)], axis=0
    ).astype(BF16)
    filtered = [None] * blocks
    for b in range(2 * blocks - 1):
        product = dot(pieces, ramp[b])
        for source in range(blocks):
            goal = source + b - (blocks - 1)
            if 0 <= goal < blocks:
                part = product[source * ar : (source + 1) * ar]
                filtered[goal] = part if filtered[goal] is None else filtered[goal] + part
    lanes = [filtered[n // 2][:, n % 2 * 128 : n % 2 * 128 + 128] for n in range(cols // 128)]

    centre = (cols - 1) / 2.0
    mags = by_row(mag, (ar, 128), angs)
    shifts = by_row(shift, (ar, 128), angs)
    projected = []
    for n in range(cols // 128):
        edges = [
            (x - centre) * m + centre + s
            for x in (n * 128, n * 128 + 127)
            for m in (MAG_LOW, MAG_HIGH)
            for s in (-SHIFT_MAX, SHIFT_MAX)
        ]
        lowest = max(int((min(edges) - 0.1) // 128), 0)
        highest = min(int((max(edges) + 1.1) // 128), cols // 128 - 1)
        places = ((iota((ar, 128), 1) + n * 128).astype(F32) - centre) * mags + centre + shifts
        floors = jnp.floor(places)
        weight = places - floors
        low = floors.astype(jnp.int32)
        ends = []
        for index in (low, low + 1):
            value = jnp.zeros((ar, 128), F32)
            for k in range(lowest, highest + 1):
                taken = jnp.take_along_axis(lanes[k], index & 127, axis=1)
                value = jnp.where(index >> 7 == k, taken, value)
            ends.append(value)
        projected.append((1.0 - weight) * ends[0] + weight * ends[1])

    halves = cols // n_ang // 128
    size = halves * ar
    for p in range(n_ang):
        sent[p] = jnp.concatenate(projected[p * halves : (p + 1) * halves], axis=0).astype(BF16)

    def block_copy(source, target, ang, row):
        return pltpu.make_async_remote_copy(
            src_ref=sent.at[ang],
            dst_ref=got.at[source],
            send_sem=send_sem.at[target],
            recv_sem=recv_sem.at[source],
            device_id=(ang, row),
            device_id_type=MESH,
        )

    def block_start(step, carry):
        target, ang, row = place_of(step)
        block_copy(me, target, ang, row).start()
        return carry

    lax.fori_loop(1, total, block_start, 0)
    got[me] = sent[my_ang]

    def frac_wait(step, carry):
        peer = lax.rem(my_ang + step, n_ang)
        frac_copy(peer, peer).wait()
        return carry

    lax.fori_loop(1, n_ang, frac_wait, 0)

    slots = order.shape[0] // n_row
    depth = total * size
    zs = slots * SLAB_Z
    place = iota((zs, depth), 1)
    level = iota((zs, depth), 0)
    source_ang = place // (n_row * size)
    piece_row = place // size % n_row * rows + place % rows
    half_of = place % size // ar
    starts = jnp.zeros((zs, depth), jnp.int32)
    fraction = jnp.zeros((zs, depth), F32)
    for p in range(n_ang):
        here = source_ang == p
        spread = jnp.concatenate([frac_all[p][0:1]] * (depth // 128), axis=1)
        fraction = jnp.where(here, jnp.broadcast_to(spread, (zs, depth)), fraction)
        for k in range(slots):
            first = offsets[p, order[my_row * slots + k]]
            starts = jnp.where(here & (level // SLAB_Z == k), first, starts)
    reach = piece_row - starts - level % SLAB_Z
    weights = jnp.where(reach == 0, 1.0 - fraction, jnp.where(reach == 1, fraction, 0.0))
    parts = []
    for h in range(halves):
        left_over = jnp.where(half_of == h, weights, 0.0)
        for _ in range(3):
            part = left_over.astype(BF16)
            left_over = left_over - part.astype(F32)
            parts.append(part)
    stacked = jnp.concatenate(parts, axis=0)

    def block_wait(step, carry):
        target, ang, row = place_of(step)
        block_copy(target, target, ang, row).wait()
        return carry

    lax.fori_loop(1, total, block_wait, 0)

    sums = dot(stacked, got[...].reshape(depth, 128))
    for h in range(halves):
        three = [sums[(h * 3 + s) * zs : (h * 3 + s + 1) * zs] for s in range(3)]
        vol_out[:, pl.ds(h * 128, 128)] = (three[2] + three[1] + three[0]) / math.sqrt(n_ang * angs)


def per_device(
    n_ang, n_row, dual_field, forward, sinogram, first_weight, first_bias, middle_weight,
    middle_bias, last_weight, magnify, detector_shift, row_fraction, offsets, slab_order,
):
    angs, rows, cols = dual_field.shape
    ch = first_weight.shape[2]
    total = n_ang * n_row
    ar = angs * rows
    out1, out2 = angs + 4, angs + 2
    blocks = cols // TILE
    width = cols // n_ang
    size = width // 128 * ar
    slots = slab_order.shape[0] // n_row
    vmem = pl.BlockSpec(memory_space=pltpu.VMEM)
    smem = pl.BlockSpec(memory_space=pltpu.SMEM)
    dma = pltpu.SemaphoreType.DMA
    return pl.pallas_call(
        functools.partial(kernel, n_ang, n_row),
        out_shape=(
            jax.ShapeDtypeStruct(dual_field.shape, BF16),
            jax.ShapeDtypeStruct((slots * SLAB_Z, width), F32),
        ),
        in_specs=[vmem] * 8 + [smem] * 5,
        out_specs=(vmem, vmem),
        scratch_shapes=[
            pltpu.VMEM((2, 3, 3, rows, cols), BF16),
            pltpu.VMEM((64, cols + 2 * PAD), F32),
            pltpu.VMEM((rows * out1 * ch, cols + 2 * PAD), F32),
            pltpu.VMEM((rows * out2 * ch, TILE), BF16),
            pltpu.VMEM((3 * ar, cols), F32),
            pltpu.VMEM((rows * out1 * ch, 3 * 64), BF16),
            pltpu.VMEM((out2 * ch, 3 * out1 * ch), BF16),
            pltpu.VMEM((3 * ar, rows * out2 * ch), F32),
            pltpu.VMEM((2 * blocks - 1, TILE, TILE), BF16),
            pltpu.VMEM((8, 128), F32),
            pltpu.VMEM((n_ang, 8, 128), F32),
            pltpu.VMEM((n_ang, size, 128), BF16),
            pltpu.VMEM((total, size, 128), BF16),
            dma((2, 3)),
            dma((2, 3)),
            dma((n_ang,)),
            dma((n_ang,)),
            dma((total,)),
            dma((total,)),
        ],
        compiler_params=pltpu.CompilerParams(
            collective_id=0, has_side_effects=True, vmem_limit_bytes=40 * 1024 * 1024
        ),
        cost_estimate=pl.CostEstimate(flops=10**9, bytes_accessed=10**6, transcendentals=0),
    )(
        dual_field, forward, sinogram, first_weight, first_bias[None, :], middle_weight,
        middle_bias[None, :], last_weight, magnify, detector_shift, row_fraction, offsets, slab_order,
    )


def solution(mesh):
    sizes = dict(mesh.shape)
    split = P("ang", "row", None)
    return jax.shard_map(
        functools.partial(per_device, sizes["ang"], sizes["row"]),
        mesh=mesh,
        in_specs=(
            split, split, split, P(), P(), P(), P(), P(), P("ang"), P("ang"), P("ang"), P(), P(),
        ),
        out_specs=(split, P("row", "ang")),
        check_vma=False,
    )
```

time: 479 us -> 31.8 us (0.07)
  local copies, waits for them, and re-layouts: 333 us -> 5.09 us
  waiting for transfers between devices: 50.1 us -> 0 us
  matrix products: 38.5 us -> 0 us
  Pallas kernels: 0 us -> 25.5 us
  blocking collectives: 16 us -> 0 us
  between operations: 14.4 us -> 0.77 us
  other arithmetic: 10.7 us -> 0 us
  starting transfers between devices: 8.89 us -> 0 us
  loops' own time: 6.17 us -> 0 us
    gather x4 -> x0, local copies, waits for them, and re-layouts: 320 us -> none  [the longest x2 160 us: interpolate(): right_vals = jnp.take_along_axis(filtered, low_index + 1, axis=2)]
    dot_general x64 -> x0, matrix products: 38.5 us -> none  [the longest x54 22.2 us: conv_taps(): jnp.einsum('oc,cau->oau', weights[ang_tap, col_tap], inputs[:, ang_tap:an...]
    reduce_scatter x1 -> x0, waiting for transfers between devices: 34.2 us -> none  [per_device(): combined = lax.psum_scatter(summed, 'ang', scatter_dimension=1, tiled=True)]
    pallas_call x0 -> x1, Pallas kernels: none -> 25.5 us  [per_device(): pl.pallas_call(functools.partial(kernel, n_ang, n_row), out_shape=(jax.Sh...]
    all_gather x1 -> x0, blocking collectives: 16 us -> none  [per_device(): row_piece = lax.all_gather(projected, 'row', axis=1, tiled=True)]
    ppermute x6 -> x0, waiting for transfers between devices: 15.8 us -> none  [the longest x3 15.8 us: extended(): before = lax.ppermute(last, axis, up)]
    ppermute x6 -> x0, starting transfers between devices: 8.85 us -> none  [the longest x3 6.1 us: extended(): after = lax.ppermute(first, axis, down)]
    another operation x4 -> x0, loops' own time: 6.17 us -> none  [the longest x1 5.61 us: per_device(): pieces = lax.map(filter_block, jnp.arange(columns // 256, dtype=jnp.int32))]
  transfers between devices with their start and end apart: 7 -> 0, of which waited for: 3 -> 0; matrix products, arithmetic and copies ran while one was open for 1% -> 0% of each run, Pallas kernels for 0% -> 0%
where the time goes in v1:
time: 31.8 us; the launch traced here: 31.4 us
  Pallas kernels  25.5 us (80%)
  local copies, waits for them, and re-layouts  5.09 us (16%)
  between operations  0.77 us (2%)
    pallas_call x1, Pallas kernels, per_device(): pl.pallas_call(functools.partial(kernel, n_ang, n_row), out_shape=(jax.Sh...  25.5 us
    unnamed x28, local copies, waits for them, and re-layouts  5.09 us

profile of v1, /device:TPU:0, one launch (start us, length us, event | category | flops | bytes accessed | tf_op | source)
XLA Modules:
  0.0 31.4 jit_solution(11830547666869013164)
XLA Ops:
  0.6 0.0 copy-start.11
  0.6 0.0 copy-start
  0.6 0.7 %copy-done.11 = bf16[3,3,1,32]{3,1,2,0:T(4,128)(2,1)S(1)} copy-done((bf16[3,3,1,32]{3,1,2,0:T(4,128)(2,1)S(1)}, bf16[3,3,1,32]{3,1,2,0:T(4,128)(2,1)}, u32[]{:S(2)}) %copy-start.11) | copy-done | bytes 600
  1.3 0.0 copy-start.6
  1.3 0.0 copy-start.7
  1.4 0.0 copy-start.8
  1.4 0.0 copy-start.9
  1.4 0.0 copy-start.10
  1.4 0.9 %copy.15.fw = bf16[3,3,32,3]{3,2,1,0:T(8,128)(2,1)S(1)} copy(bf16[3,3,32,3]{2,3,1,0:T(4,128)(2,1)} %param.16) | data formatting | bytes 3456 | tf_op args[3]
  2.3 0.0 copy-done
  2.3 0.0 copy-done.4
  2.3 0.0 copy-done.5
  2.3 0.0 copy-done.6
  2.3 0.0 copy-done.7
  2.3 0.0 copy-done.8
  2.3 0.0 copy-done.9
  2.3 0.0 copy-done.10
  2.4 0.0 copy-start.1
  2.4 0.7 %copy-done.1 = bf16[4,2,2048]{2,1,0:T(2,128)(2,1)S(1)} copy-done((bf16[4,2,2048]{2,1,0:T(2,128)(2,1)S(1)}, bf16[4,2,2048]{2,1,0:T(2,128)(2,1)}, u32[]{:S(2)}) %copy-start.1) | copy-done | bytes 32792
  3.1 0.8 %copy-done.2 = bf16[4,2,2048]{2,1,0:T(2,128)(2,1)S(1)} copy-done((bf16[4,2,2048]{2,1,0:T(2,128)(2,1)S(1)}, bf16[4,2,2048]{2,1,0:T(2,128)(2,1)}, u32[]{:S(2)}) %copy-start.2) | copy-done | bytes 32792
  3.9 0.8 %copy-done.3 = bf16[4,2,2048]{2,1,0:T(2,128)(2,1)S(1)} copy-done((bf16[4,2,2048]{2,1,0:T(2,128)(2,1)S(1)}, bf16[4,2,2048]{2,1,0:T(2,128)(2,1)}, u32[]{:S(2)}) %copy-start.3) | copy-done | bytes 32792
  4.6 25.5 %shard_map.140 = (bf16[4,2,2048]{2,1,0:T(2,128)(2,1)S(1)}, f32[16,256]{1,0:T(8,128)S(1)}) custom-call(bf16[4,2,2048]{2,1,0:T(2,128)(2,1)S(1)} %copy-done.1, bf16[4,2,2048]{2,1,0:T(2,128)(2,1)S(1)} %copy-done.2, bf16[4,2,2048]{2,1,0:T(2,128)(2,1)S(1)} %copy-done.3, bf16[3,3,32,3]{3,2,1,0:T(8,128)(2,1)S(1)} %copy.15.fw, f32[1,32]{1,0:T(1,128)S(1)} %bitcast.2, ...), custom_call_target="tpu_custom_call" | custom-call | flops 1000000000 | bytes 1000000 | tf_op jit(solution)/shard_map/pallas_call | solution.py:350
  30.2 0.6 %copy.19 = bf16[4,2,2048]{2,1,0:T(2,128)(2,1)} copy(bf16[4,2,2048]{2,1,0:T(2,128)(2,1)S(1)} %get-tuple-element.4) | data formatting | bytes 65536
  30.8 0.6 %copy.20 = f32[16,256]{1,0:T(8,128)} copy(f32[16,256]{1,0:T(8,128)S(1)} %get-tuple-element.5) | data formatting | bytes 32768
  (5 shorter events, 0.0 us)
Async XLA Ops:
  0.6 0.7 %copy-start.11 = (bf16[3,3,1,32]{3,1,2,0:T(4,128)(2,1)S(1)}, bf16[3,3,1,32]{3,1,2,0:T(4,128)(2,1)}, u32[]{:S(2)}) copy-start(bf16[3,3,1,32]{3,1,2,0:T(4,128)(2,1)} %param.20) | copy-start | bytes 1732
  0.6 1.6 %copy-start = (bf16[3,3,32,32]{3,2,1,0:T(8,128)(2,1)S(1)}, bf16[3,3,32,32]{3,2,1,0:T(8,128)(2,1)}, u32[]{:S(2)}) copy-start(bf16[3,3,32,32]{3,2,1,0:T(8,128)(2,1)} %mw.1) | copy-start | bytes 55300
  1.3 1.0 %copy-start.4 = (s32[8,16]{1,0:T(8,128)S(1)}, s32[8,16]{1,0:T(8,128)}, u32[]{:S(2)}) copy-start(s32[8,16]{1,0:T(8,128)} %offsets.1) | copy-start | bytes 1540
  1.3 1.0 %copy-start.5 = (f32[32]{0:T(128)S(1)}, f32[32]{0:T(128)}, u32[]{:S(2)}) copy-start(f32[32]{0:T(128)} %param.17) | copy-start | bytes 388
  1.3 1.0 %copy-start.6 = (f32[32]{0:T(128)S(1)}, f32[32]{0:T(128)}, u32[]{:S(2)}) copy-start(f32[32]{0:T(128)} %param.19) | copy-start | bytes 388
  1.3 1.0 %copy-start.7 = (f32[4]{0:T(128)S(1)}, f32[4]{0:T(128)}, u32[]{:S(2)}) copy-start(f32[4]{0:T(128)} %mag.1) | copy-start | bytes 52
  1.4 1.0 %copy-start.8 = (f32[4]{0:T(128)S(1)}, f32[4]{0:T(128)}, u32[]{:S(2)}) copy-start(f32[4]{0:T(128)} %shift.1) | copy-start | bytes 52
  1.4 1.0 %copy-start.9 = (f32[4]{0:T(128)S(1)}, f32[4]{0:T(128)}, u32[]{:S(2)}) copy-start(f32[4]{0:T(128)} %frac.1) | copy-start | bytes 52
  1.4 1.0 %copy-start.10 = (s32[16]{0:T(128)S(1)}, s32[16]{0:T(128)}, u32[]{:S(2)}) copy-start(s32[16]{0:T(128)} %order.1) | copy-start | bytes 196
  2.4 0.8 %copy-start.1 = (bf16[4,2,2048]{2,1,0:T(2,128)(2,1)S(1)}, bf16[4,2,2048]{2,1,0:T(2,128)(2,1)}, u32[]{:S(2)}) copy-start(bf16[4,2,2048]{2,1,0:T(2,128)(2,1)} %dual.1) | copy-start | bytes 98308
  3.1 0.8 %copy-start.2 = (bf16[4,2,2048]{2,1,0:T(2,128)(2,1)S(1)}, bf16[4,2,2048]{2,1,0:T(2,128)(2,1)}, u32[]{:S(2)}) copy-start(bf16[4,2,2048]{2,1,0:T(2,128)(2,1)} %forward.1) | copy-start | bytes 98308
  3.9 0.8 %copy-start.3 = (bf16[4,2,2048]{2,1,0:T(2,128)(2,1)S(1)}, bf16[4,2,2048]{2,1,0:T(2,128)(2,1)}, u32[]{:S(2)}) copy-start(bf16[4,2,2048]{2,1,0:T(2,128)(2,1)} %sino.1) | copy-start | bytes 98308

commit v2 on v1

--- a/solution.py
+++ b/solution.py
@@ -10,7 +10,6 @@
 
 SLAB_Z = 4
 MAG_LOW, MAG_HIGH, SHIFT_MAX = 0.85, 0.95, 8.0
-PAD = 128
 TILE = 256
 F32 = jnp.float32
 BF16 = jnp.bfloat16
@@ -46,22 +45,44 @@
     return value
 
 
-def shifted(window, width):
-    size = window.shape[1]
-    left = pltpu.roll(window, 1, 1)[:, PAD : PAD + width]
-    right = pltpu.roll(window, size - 1, 1)[:, PAD : PAD + width]
-    mid = window[:, PAD : PAD + width]
-    return jnp.concatenate([left.astype(BF16), mid.astype(BF16), right.astype(BF16)], axis=0)
+def log2(size):
+    assert size & (size - 1) == 0
+    return size.bit_length() - 1
+
+
+def split(value, size, count):
+    quotient = jnp.zeros_like(value)
+    for k in range(1, count):
+        quotient = quotient + jnp.where(value >= k * size, 1, 0)
+    return quotient, value - quotient * size
+
+
+def shifted(values):
+    cols = values.shape[1]
+    column = iota(values.shape, 1)
+    zero = jnp.zeros_like(values)
+    before = jnp.where(column == 0, zero, pltpu.roll(values, 1, 1))
+    after = jnp.where(column == cols - 1, zero, pltpu.roll(values, cols - 1, 1))
+    return before, after
 
 
 def kernel(
-    n_ang, n_row, dual, forward, sino, fw, fb, mw, mb, lw, mag, shift, frac, offsets, order,
-    nd_out, vol_out,
-    halo, x1, x2, x3, taps, w1, w2, w3, ramp, frac_own, frac_all, sent, got,
-    halo_send, halo_recv, frac_send, frac_recv, send_sem, recv_sem,
+    n_ang, n_row, *refs,
 ):
+    sources, (nd_out, vol_out), locals_ = refs[:13], refs[13:15], refs[15:28]
+    dual, forward, sino, fw, fb, mw, mb, lw, mag, shift, frac, offsets, order = locals_
+    (
+    halo, x1, x1s, x2, x3, taps, w1, w2, w3, ramp, frac_own, frac_all, sent, got,
+    halo_send, halo_recv, frac_send, frac_recv, send_sem, recv_sem, local_sem,
+    ) = refs[28:]
+    loads = [
+        pltpu.make_async_copy(source, goal, local_sem.at[n])
+        for n, (source, goal) in enumerate(zip(sources, locals_))
+    ]
+    for load in loads:
+        load.start()
     angs, rows, cols = dual.shape
-    ch = fw.shape[2]
+    ch = mw.shape[2]
     total = n_ang * n_row
     my_ang, my_row = lax.axis_index("ang"), lax.axis_index("row")
     me = my_ang * n_row + my_row
@@ -83,18 +104,23 @@
 
     lax.fori_loop(1, total, greet, 0)
 
-    lane = iota((8, 128), 1)
-    mine = jnp.full((8, 128), frac[0], F32)
-    for a in range(1, angs):
-        mine = jnp.where((lane // rows) % angs == a, frac[a], mine)
-    frac_own[...] = mine
-    frac_all[my_ang] = mine
+    narrow = cols // 128
+
+    def ramp_block(b, carry):
+        away = (b - (narrow - 1)) * 128 + iota((128, 128), 1) - iota((128, 128), 0)
+        odd = (away & 1) == 1
+        distance = jnp.where(odd, away, 1).astype(F32)
+        value = jnp.where(odd, -1.0 / (math.pi * math.pi * distance * distance), 0.0)
+        ramp[:, pl.ds(pl.multiple_of(b * 128, 128), 128)] = jnp.where(away == 0, 0.25, value).astype(BF16)
+        return carry
+
+    lax.fori_loop(0, 2 * narrow - 1, ramp_block, 0)
     pl.semaphore_wait(barrier, total - 1)
 
     left = lax.rem(my_ang + n_ang - 1, n_ang)
     right = lax.rem(my_ang + 1, n_ang)
     halo_copies = []
-    for c, ref in enumerate((dual, forward, sino)):
+    for c, ref in enumerate(sources[:3]):
         for side, (peer, first) in enumerate(((right, angs - 3), (left, 0))):
             copy = pltpu.make_async_remote_copy(
                 src_ref=ref.at[pl.ds(first, 3)],
@@ -107,6 +133,15 @@
             copy.start()
             halo_copies.append(copy)
 
+    for load in loads:
+        load.wait()
+    lane = iota((8, 128), 1)
+    mine = jnp.full((8, 128), frac[0], F32)
+    for a in range(1, angs):
+        mine = jnp.where((lane & (ar - 1)) // rows == a, frac[a], mine)
+    frac_own[...] = mine
+    frac_all[my_ang] = mine
+
     def frac_copy(source, target):
         return pltpu.make_async_remote_copy(
             src_ref=frac_own,
@@ -124,13 +159,18 @@
     lax.fori_loop(1, n_ang, frac_start, 0)
 
     k1 = 3 * per
-    pick1 = iota((3, k1), 1) % per // (wide * rows) == iota((3, k1), 0)
-    pick1 = jnp.where(pick1, 1.0, 0.0).astype(BF16)
-    place1 = iota((ch, k1), 1)
-    tap1, rest1 = place1 // per, place1 % per
-    ang1 = jnp.where(rest1 < 3 * wide * rows, rest1 % (wide * rows) // rows, -9)
-    row1 = rest1 % rows
-    tiles1 = [[dot(fw[i, j], pick1) for j in range(3)] for i in range(3)]
+    tap1, rest1 = split(iota((ch, k1), 1), per, 3)
+    chan1, rest1 = split(rest1, wide * rows, 4)
+    ang1 = jnp.where(chan1 < 3, rest1 >> 1, -9)
+    row1 = rest1 & 1
+    pick1 = jnp.where(chan1[0:3] == iota((3, k1), 0), 1.0, 0.0).astype(BF16)
+    tiles1 = [
+        [
+            lax.dot_general(fw[i, j], pick1, (((0,), (0,)), ((), ())), preferred_element_type=F32)
+            for j in range(3)
+        ]
+        for i in range(3)
+    ]
     joined1 = [
         jnp.where(tap1 == 0, tiles1[i][0], jnp.where(tap1 == 1, tiles1[i][1], tiles1[i][2]))
         for i in range(3)
@@ -143,8 +183,8 @@
             w1[pl.ds((r * out1 + a) * ch, ch), :] = block.astype(BF16)
 
     k2 = out1 * ch
-    pick2 = jnp.where(iota((ch, k2), 1) % ch == iota((ch, k2), 0), 1.0, 0.0).astype(BF16)
-    ang2 = iota((ch, k2), 1) // ch
+    pick2 = jnp.where((iota((ch, k2), 1) & (ch - 1)) == iota((ch, k2), 0), 1.0, 0.0).astype(BF16)
+    ang2, _ = split(iota((ch, k2), 1), ch, out1)
     for j in range(3):
         tiles2 = [dot(mw[i, j], pick2) for i in range(3)]
         for a in range(out2):
@@ -154,85 +194,94 @@
             w2[pl.ds(a * ch, ch), pl.ds(j * k2, k2)] = block.astype(BF16)
 
     k3 = rows * out2 * ch
-    pick3 = jnp.where(iota((ch, k3), 1) % ch == iota((ch, k3), 0), 1.0, 0.0).astype(BF16)
-    place3 = iota((ar, k3), 1)
-    ang3 = place3 // ch % out2 - iota((ar, k3), 0) // rows
-    same3 = place3 // (out2 * ch) == iota((ar, k3), 0) % rows
+    pick3 = jnp.where((iota((ch, k3), 1) & (ch - 1)) == iota((ch, k3), 0), 1.0, 0.0).astype(BF16)
+    row3, rest3 = split(iota((ar, k3), 1), out2 * ch, rows)
+    ang3, _ = split(rest3, ch, out2)
+    ang3 = ang3 - (iota((ar, k3), 0) >> 1)
+    same3 = row3 == (iota((ar, k3), 0) & 1)
+    blocks3 = []
     for j in range(3):
         block = jnp.zeros((ar, k3), F32)
         for i in range(3):
-            weights = jnp.broadcast_to(lw[i, j].astype(F32), (ar, ch)).astype(BF16)
+            weights = jnp.broadcast_to(lw[i, 0, j : j + 1, :].astype(F32), (ar, ch)).astype(BF16)
             block = jnp.where((ang3 == i) & same3, dot(weights, pick3), block)
-        w3[pl.ds(j * ar, ar), :] = block
-
-    blocks = cols // TILE
-
-    def ramp_block(b, carry):
-        away = (b - (blocks - 1)) * TILE + iota((TILE, TILE), 1) - iota((TILE, TILE), 0)
-        odd = away % 2 == 1
-        distance = jnp.where(odd, away, 1).astype(F32)
-        value = jnp.where(odd, -1.0 / (math.pi * math.pi * distance * distance), 0.0)
-        ramp[b] = jnp.where(away == 0, 0.25, value).astype(BF16)
-        return carry
-
-    lax.fori_loop(0, 2 * blocks - 1, ramp_block, 0)
+        blocks3.append(block)
+    blocks3.append(jnp.zeros((ar, k3), F32))
+    w3[...] = jnp.concatenate(blocks3, axis=0).astype(BF16)
 
     bias1 = jnp.concatenate([as_column(fb[...])] * (rows * out1), axis=0)
     bias2 = jnp.concatenate([as_column(mb[...])] * out2, axis=0)
 
     x1[...] = jnp.zeros_like(x1)
-    x2[:, pl.ds(0, PAD)] = jnp.zeros((x2.shape[0], PAD), F32)
-    x2[:, pl.ds(PAD + cols, PAD)] = jnp.zeros((x2.shape[0], PAD), F32)
     for c, ref in enumerate((dual, forward, sino)):
         for a in range(angs):
-            x1[pl.ds((c * wide + 3 + a) * rows, rows), pl.ds(PAD, cols)] = ref[a].astype(F32)
+            x1[pl.ds((c * wide + 3 + a) * rows, rows), :] = ref[a].astype(F32)
     for copy in halo_copies:
         copy.wait()
     for c in range(3):
         for a in range(3):
-            x1[pl.ds((c * wide + a) * rows, rows), pl.ds(PAD, cols)] = halo[0, c, a].astype(F32)
-            x1[pl.ds((c * wide + 3 + angs + a) * rows, rows), pl.ds(PAD, cols)] = halo[1, c, a].astype(F32)
+            x1[pl.ds((c * wide + a) * rows, rows), :] = halo[0, c, a].astype(F32)
+            x1[pl.ds((c * wide + 3 + angs + a) * rows, rows), :] = halo[1, c, a].astype(F32)
+    middle = x1[...].astype(BF16)
+    before, after = shifted(middle)
+    x1s[pl.ds(0, per), :] = before
+    x1s[pl.ds(per, per), :] = middle
+    x1s[pl.ds(2 * per, per), :] = after
+    tiles = cols // TILE
 
     def layer1(t, carry):
         start = pl.multiple_of(t * TILE, TILE)
-        stack = shifted(x1[:, pl.ds(start, TILE + 2 * PAD)], TILE)
-        x2[:, pl.ds(start + PAD, TILE)] = silu(dot(w1[...], stack) + bias1)
-        return carry
-
-    lax.fori_loop(0, blocks, layer1, 0)
+        value = silu(dot(w1[...], x1s[:, pl.ds(start, TILE)]) + bias1).astype(BF16)
+        for r in range(rows):
+            x2[pl.ds((r * 3 + 1) * k2, k2), pl.ds(start, TILE)] = value[r * k2 : (r + 1) * k2]
+        return carry
+
+    lax.fori_loop(0, tiles, layer1, 0)
+
+    def shift2(n, carry):
+        for r in range(rows):
+            base = r * 3 * k2 + n * ch
+            values = x2[pl.ds(pl.multiple_of(base + k2, ch), ch), :]
+            before, after = shifted(values)
+            x2[pl.ds(pl.multiple_of(base, ch), ch), :] = before
+            x2[pl.ds(pl.multiple_of(base + 2 * k2, ch), ch), :] = after
+        return carry
+
+    lax.fori_loop(0, out1, shift2, 0)
 
     def layer2(t, carry):
         start = pl.multiple_of(t * TILE, TILE)
         for r in range(rows):
-            stack = shifted(x2[pl.ds(r * k2, k2), pl.ds(start, TILE + 2 * PAD)], TILE)
-            value = silu(dot(w2[...], stack) + bias2)
+            value = silu(dot(w2[...], x2[pl.ds(r * 3 * k2, 3 * k2), pl.ds(start, TILE)]) + bias2)
             x3[pl.ds(r * out2 * ch, out2 * ch), :] = value.astype(BF16)
-        taps[:, pl.ds(start, TILE)] = dot(w3[...].astype(BF16), x3[...])
-        return carry
-
-    lax.fori_loop(0, blocks, layer2, 0)
+        taps[:, pl.ds(start, TILE)] = dot(w3[...], x3[...])[0 : 3 * ar]
+        return carry
+
+    lax.fori_loop(0, tiles, layer2, 0)
 
     column = iota((ar, cols), 1)
     before = jnp.where(column == 0, 0.0, pltpu.roll(taps[0:ar, :], 1, 1))
     after = jnp.where(column == cols - 1, 0.0, pltpu.roll(taps[2 * ar : 3 * ar, :], cols - 1, 1))
     update = before + taps[ar : 2 * ar, :] + after
-    own = x1[pl.ds(3 * rows, ar), pl.ds(PAD, cols)]
+    own = x1[pl.ds(3 * rows, ar), :]
     new_dual = (own + update).astype(BF16).astype(F32)
     for a in range(angs):
         nd_out[a] = new_dual[a * rows : (a + 1) * rows].astype(BF16)
 
     pieces = jnp.concatenate(
-        [new_dual[:, b * TILE : (b + 1) * TILE] for b in range(blocks)], axis=0
+        [new_dual[:, n * 128 : (n + 1) * 128] for n in range(narrow)], axis=0
     ).astype(BF16)
-    filtered = [None] * blocks
-    for b in range(2 * blocks - 1):
-        product = dot(pieces, ramp[b])
-        for source in range(blocks):
-            goal = source + b - (blocks - 1)
-            if 0 <= goal < blocks:
-                part = product[source * ar : (source + 1) * ar]
-                filtered[goal] = part if filtered[goal] is None else filtered[goal] + part
-    lanes = [filtered[n // 2][:, n % 2 * 128 : n % 2 * 128 + 128] for n in range(cols // 128)]
+    lanes = [None] * narrow
+    for pair in range(0, 2 * narrow - 1, 2):
+        near = min(2, 2 * narrow - 1 - pair)
+        product = dot(pieces, ramp[:, pl.ds(pair * 128, near * 128)])
+        for b in range(pair, pair + near):
+            for source in range(narrow):
+                goal = source + b - (narrow - 1)
+                if 0 <= goal < narrow:
+                    at = (b - pair) * 128
+                    part = product[source * ar : (source + 1) * ar, at : at + 128]
+                    lanes[goal] = part if lanes[goal] is None else lanes[goal] + part
 
     centre = (cols - 1) / 2.0
     mags = by_row(mag, (ar, 128), angs)
@@ -295,9 +344,9 @@
     zs = slots * SLAB_Z
     place = iota((zs, depth), 1)
     level = iota((zs, depth), 0)
-    source_ang = place // (n_row * size)
-    piece_row = place // size % n_row * rows + place % rows
-    half_of = place % size // ar
+    source_ang = (place >> log2(n_row * size))
+    piece_row = ((place >> log2(size)) & (n_row - 1)) * rows + (place & (rows - 1))
+    half_of = ((place & (size - 1)) >> log2(ar))
     starts = jnp.zeros((zs, depth), jnp.int32)
     fraction = jnp.zeros((zs, depth), F32)
     for p in range(n_ang):
@@ -306,8 +355,8 @@
         fraction = jnp.where(here, jnp.broadcast_to(spread, (zs, depth)), fraction)
         for k in range(slots):
             first = offsets[p, order[my_row * slots + k]]
-            starts = jnp.where(here & (level // SLAB_Z == k), first, starts)
-    reach = piece_row - starts - level % SLAB_Z
+            starts = jnp.where(here & ((level >> log2(SLAB_Z)) == k), first, starts)
+    reach = piece_row - starts - (level & (SLAB_Z - 1))
     weights = jnp.where(reach == 0, 1.0 - fraction, jnp.where(reach == 1, fraction, 0.0))
     parts = []
     for h in range(halves):
@@ -337,15 +386,19 @@
 ):
     angs, rows, cols = dual_field.shape
     ch = first_weight.shape[2]
+    operands = (
+        dual_field, forward, sinogram, first_weight.transpose(0, 1, 3, 2), first_bias[None, :],
+        middle_weight, middle_bias[None, :], last_weight.transpose(0, 2, 1, 3), magnify,
+        detector_shift, row_fraction, offsets, slab_order,
+    )
     total = n_ang * n_row
     ar = angs * rows
     out1, out2 = angs + 4, angs + 2
-    blocks = cols // TILE
+    narrow = cols // 128
     width = cols // n_ang
     size = width // 128 * ar
     slots = slab_order.shape[0] // n_row
     vmem = pl.BlockSpec(memory_space=pltpu.VMEM)
-    smem = pl.BlockSpec(memory_space=pltpu.SMEM)
     dma = pltpu.SemaphoreType.DMA
     return pl.pallas_call(
         functools.partial(kernel, n_ang, n_row),
@@ -353,18 +406,21 @@
             jax.ShapeDtypeStruct(dual_field.shape, BF16),
             jax.ShapeDtypeStruct((slots * SLAB_Z, width), F32),
         ),
-        in_specs=[vmem] * 8 + [smem] * 5,
+        in_specs=[pl.BlockSpec(memory_space=pltpu.HBM)] * 13,
         out_specs=(vmem, vmem),
-        scratch_shapes=[
+        scratch_shapes=[pltpu.VMEM(x.shape, x.dtype) for x in operands[:8]]
+        + [pltpu.SMEM(x.shape, x.dtype) for x in operands[8:]]
+        + [
             pltpu.VMEM((2, 3, 3, rows, cols), BF16),
-            pltpu.VMEM((64, cols + 2 * PAD), F32),
-            pltpu.VMEM((rows * out1 * ch, cols + 2 * PAD), F32),
+            pltpu.VMEM((64, cols), F32),
+            pltpu.VMEM((3 * 64, cols), BF16),
+            pltpu.VMEM((rows * 3 * out1 * ch, cols), BF16),
             pltpu.VMEM((rows * out2 * ch, TILE), BF16),
             pltpu.VMEM((3 * ar, cols), F32),
             pltpu.VMEM((rows * out1 * ch, 3 * 64), BF16),
             pltpu.VMEM((out2 * ch, 3 * out1 * ch), BF16),
-            pltpu.VMEM((3 * ar, rows * out2 * ch), F32),
-            pltpu.VMEM((2 * blocks - 1, TILE, TILE), BF16),
+            pltpu.VMEM((4 * ar, rows * out2 * ch), BF16),
+            pltpu.VMEM((128, (2 * narrow - 1) * 128), BF16),
             pltpu.VMEM((8, 128), F32),
             pltpu.VMEM((n_ang, 8, 128), F32),
             pltpu.VMEM((n_ang, size, 128), BF16),
@@ -375,15 +431,13 @@
             dma((n_ang,)),
             dma((total,)),
             dma((total,)),
+            dma((13,)),
         ],
         compiler_params=pltpu.CompilerParams(
-            collective_id=0, has_side_effects=True, vmem_limit_bytes=40 * 1024 * 1024
+            collective_id=0, has_side_effects=True, vmem_limit_bytes=65280 * 1024
         ),
         cost_estimate=pl.CostEstimate(flops=10**9, bytes_accessed=10**6, transcendentals=0),
-    )(
-        dual_field, forward, sinogram, first_weight, first_bias[None, :], middle_weight,
-        middle_bias[None, :], last_weight, magnify, detector_shift, row_fraction, offsets, slab_order,
-    )
+    )(*operands)
 
 
 def solution(mesh):

time: 31.8 us -> 29.5 us (0.928)
  local copies, waits for them, and re-layouts: 5.09 us -> 2.01 us
  Pallas kernels: 25.5 us -> 26.7 us
    unnamed x28 -> x4, local copies, waits for them, and re-layouts: 5.09 us -> 2.01 us
    pallas_call x1, Pallas kernels: 25.5 us -> 26.7 us  [per_device(): pl.pallas_call(functools.partial(kernel, n_ang, n_row), out_shape=(jax.Sh...]
where the time goes in v2:
time: 29.5 us; the launch traced here: 29.4 us
  Pallas kernels  26.7 us (91%)
  local copies, waits for them, and re-layouts  2.01 us (7%)
  between operations  0.65 us (2%)
    pallas_call x1, Pallas kernels, per_device(): pl.pallas_call(functools.partial(kernel, n_ang, n_row), out_shape=(jax.Sh...  26.7 us
    unnamed x4, local copies, waits for them, and re-layouts  2.01 us

profile of v2, /device:TPU:0, one launch (start us, length us, event | category | flops | bytes accessed | tf_op | source)
XLA Modules:
  0.0 29.4 jit_solution(6023413496298123631)
XLA Ops:
  0.6 26.7 %shard_map.140 = (bf16[4,2,2048]{2,1,0:T(2,128)(2,1)}, f32[16,256]{1,0:T(8,128)}) custom-call(bf16[4,2,2048]{2,1,0:T(2,128)(2,1)} %refs_0_.1, bf16[4,2,2048]{2,1,0:T(2,128)(2,1)} %refs_1_.1, bf16[4,2,2048]{2,1,0:T(2,128)(2,1)} %refs_2_.1, bf16[3,3,3,32]{3,2,1,0:T(4,128)(2,1)} %bitcast.4, f32[1,32]{1,0:T(1,128)} %bitcast.6, bf16[3,3,32,32]{3,2,1,0:T(8,128)(2,1)} %refs_5_.1, ...), custom_call_target="tpu_custom_call" | custom-call | flops 1000000000 | bytes 1000000 | tf_op jit(solution)/shard_map/pallas_call | solution.py:403
  27.3 0.0 copy-start
  27.3 1.4 %copy.17 = bf16[4,2,2048]{2,1,0:T(2,128)(2,1)} copy(bf16[4,2,2048]{2,1,0:T(2,128)(2,1)} %get-tuple-element.4) | data formatting | bytes 65536
  28.7 0.0 copy-done
  28.7 0.6 %copy.18 = f32[16,256]{1,0:T(8,128)} copy(f32[16,256]{1,0:T(8,128)S(1)} %copy-done) | data formatting | bytes 32768
Async XLA Ops:
  27.3 1.4 %copy-start = (f32[16,256]{1,0:T(8,128)S(1)}, f32[16,256]{1,0:T(8,128)}, u32[]{:S(2)}) copy-start(f32[16,256]{1,0:T(8,128)} %get-tuple-element.5) | copy-start | bytes 49156

commit v3 on v2

--- a/solution.py
+++ b/solution.py
@@ -10,7 +10,7 @@
 
 SLAB_Z = 4
 MAG_LOW, MAG_HIGH, SHIFT_MAX = 0.85, 0.95, 8.0
-TILE = 256
+TILE = 512
 F32 = jnp.float32
 BF16 = jnp.bfloat16
 MESH = pl.DeviceIdType.MESH
@@ -20,8 +20,7 @@
     return jnp.dot(a, b, preferred_element_type=F32)
 
 
-def silu(v):
-    half = 0.5 * v
+def silu_of_half(half):
     return half + half * jnp.tanh(half)
 
 
@@ -57,13 +56,18 @@
     return quotient, value - quotient * size
 
 
-def shifted(values):
+def store_shifted(ref, first_before, first_after, count, values):
     cols = values.shape[1]
-    column = iota(values.shape, 1)
-    zero = jnp.zeros_like(values)
-    before = jnp.where(column == 0, zero, pltpu.roll(values, 1, 1))
-    after = jnp.where(column == cols - 1, zero, pltpu.roll(values, cols - 1, 1))
-    return before, after
+    column = iota((count, 128), 1)
+    zero = jnp.zeros((count, 128), values.dtype)
+    before = pltpu.roll(values, 1, 1)
+    after = pltpu.roll(values, cols - 1, 1)
+    ref[pl.ds(first_before, count), pl.ds(128, cols - 128)] = before[:, 128:]
+    ref[pl.ds(first_before, count), pl.ds(0, 128)] = jnp.where(column == 0, zero, before[:, :128])
+    ref[pl.ds(first_after, count), pl.ds(0, cols - 128)] = after[:, : cols - 128]
+    ref[pl.ds(first_after, count), pl.ds(cols - 128, 128)] = jnp.where(
+        column == 127, zero, after[:, cols - 128 :]
+    )
 
 
 def kernel(
@@ -72,7 +76,7 @@
     sources, (nd_out, vol_out), locals_ = refs[:13], refs[13:15], refs[15:28]
     dual, forward, sino, fw, fb, mw, mb, lw, mag, shift, frac, offsets, order = locals_
     (
-    halo, x1, x1s, x2, x3, taps, w1, w2, w3, ramp, frac_own, frac_all, sent, got,
+    halo, x1, x1s, x2, x3, wrows, w1, w2, w3, ramp, frac_own, frac_all, sent, got,
     halo_send, halo_recv, frac_send, frac_recv, send_sem, recv_sem, local_sem,
     ) = refs[28:]
     loads = [
@@ -106,15 +110,13 @@
 
     narrow = cols // 128
 
-    def ramp_block(b, carry):
+    def ramp_block(b):
         away = (b - (narrow - 1)) * 128 + iota((128, 128), 1) - iota((128, 128), 0)
         odd = (away & 1) == 1
         distance = jnp.where(odd, away, 1).astype(F32)
         value = jnp.where(odd, -1.0 / (math.pi * math.pi * distance * distance), 0.0)
         ramp[:, pl.ds(pl.multiple_of(b * 128, 128), 128)] = jnp.where(away == 0, 0.25, value).astype(BF16)
-        return carry
-
-    lax.fori_loop(0, 2 * narrow - 1, ramp_block, 0)
+
     pl.semaphore_wait(barrier, total - 1)
 
     left = lax.rem(my_ang + n_ang - 1, n_ang)
@@ -163,30 +165,39 @@
     chan1, rest1 = split(rest1, wide * rows, 4)
     ang1 = jnp.where(chan1 < 3, rest1 >> 1, -9)
     row1 = rest1 & 1
-    pick1 = jnp.where(chan1[0:3] == iota((3, k1), 0), 1.0, 0.0).astype(BF16)
-    tiles1 = [
-        [
-            lax.dot_general(fw[i, j], pick1, (((0,), (0,)), ((), ())), preferred_element_type=F32)
-            for j in range(3)
-        ]
-        for i in range(3)
-    ]
-    joined1 = [
-        jnp.where(tap1 == 0, tiles1[i][0], jnp.where(tap1 == 1, tiles1[i][1], tiles1[i][2]))
-        for i in range(3)
-    ]
+    for i in range(3):
+        for j in range(3):
+            wrows[pl.ds((i * 3 + j) * 3, 3), :] = fw[i, j].astype(F32)
+    entry = iota((32, 4 * per), 0)
+    tap_all, rest_all = split(iota((32, 4 * per), 1), per, 4)
+    chan_all, _ = split(rest_all, wide * rows, 4)
+    chosen = jnp.where(chan_all < 3, tap_all * 3 + chan_all, -99)
+    chosen = jnp.where(tap_all < 3, chosen, -99)
+    pick1 = jnp.concatenate(
+        [jnp.where(entry == chosen + i * 9, 0.5, 0.0).astype(BF16) for i in range(3)], axis=1
+    )
+    entries = jnp.where(iota((32, ch), 0) < 27, wrows[...], 0.0).astype(BF16)
+    tiles1 = lax.dot_general(entries, pick1, (((0,), (0,)), ((), ())), preferred_element_type=F32)
+    joined1 = [tiles1[:, i * 4 * per : i * 4 * per + k1] for i in range(3)]
+    bias1 = jnp.zeros((ch, k1), F32)
+    left_over = as_column(fb[...]) * 0.5
+    for n in range(3):
+        part = left_over.astype(BF16).astype(F32)
+        left_over = left_over - part
+        bias1 = jnp.where(iota((ch, k1), 1) == per + 3 * wide * rows + n, part, bias1)
     for r in range(rows):
         for a in range(out1):
-            block = jnp.zeros((ch, k1), F32)
+            block = bias1
             for i in range(3):
                 block = jnp.where((ang1 == a + i) & (row1 == r), joined1[i], block)
             w1[pl.ds((r * out1 + a) * ch, ch), :] = block.astype(BF16)
 
     k2 = out1 * ch
-    pick2 = jnp.where((iota((ch, k2), 1) & (ch - 1)) == iota((ch, k2), 0), 1.0, 0.0).astype(BF16)
+    pick2 = jnp.where((iota((ch, k2), 1) & (ch - 1)) == iota((ch, k2), 0), 0.5, 0.0).astype(BF16)
     ang2, _ = split(iota((ch, k2), 1), ch, out1)
+    all2 = dot(mw[...].reshape(9 * ch, ch), pick2)
     for j in range(3):
-        tiles2 = [dot(mw[i, j], pick2) for i in range(3)]
+        tiles2 = [all2[(i * 3 + j) * ch : (i * 3 + j + 1) * ch] for i in range(3)]
         for a in range(out2):
             block = jnp.zeros((ch, k2), F32)
             for i in range(3):
@@ -199,20 +210,24 @@
     ang3, _ = split(rest3, ch, out2)
     ang3 = ang3 - (iota((ar, k3), 0) >> 1)
     same3 = row3 == (iota((ar, k3), 0) & 1)
+    spread3 = [
+        jnp.broadcast_to(lw[i, 0, j : j + 1, :].astype(F32), (ar, ch)) for i in range(3) for j in range(3)
+    ]
+    all3 = dot(jnp.concatenate(spread3, axis=0).astype(BF16), pick3)
     blocks3 = []
     for j in range(3):
         block = jnp.zeros((ar, k3), F32)
         for i in range(3):
-            weights = jnp.broadcast_to(lw[i, 0, j : j + 1, :].astype(F32), (ar, ch)).astype(BF16)
-            block = jnp.where((ang3 == i) & same3, dot(weights, pick3), block)
+            at = (i * 3 + j) * ar
+            block = jnp.where((ang3 == i) & same3, all3[at : at + ar], block)
         blocks3.append(block)
     blocks3.append(jnp.zeros((ar, k3), F32))
     w3[...] = jnp.concatenate(blocks3, axis=0).astype(BF16)
 
-    bias1 = jnp.concatenate([as_column(fb[...])] * (rows * out1), axis=0)
-    bias2 = jnp.concatenate([as_column(mb[...])] * out2, axis=0)
-
-    x1[...] = jnp.zeros_like(x1)
+    bias2 = jnp.concatenate([as_column(mb[...]) * 0.5] * out2, axis=0)
+
+    used = 3 * wide * rows
+    x1[pl.ds(per - 8, 8), :] = jnp.where(iota((8, cols), 0) + per - 8 < used + 3, 1.0, 0.0)
     for c, ref in enumerate((dual, forward, sino)):
         for a in range(angs):
             x1[pl.ds((c * wide + 3 + a) * rows, rows), :] = ref[a].astype(F32)
@@ -223,15 +238,13 @@
             x1[pl.ds((c * wide + a) * rows, rows), :] = halo[0, c, a].astype(F32)
             x1[pl.ds((c * wide + 3 + angs + a) * rows, rows), :] = halo[1, c, a].astype(F32)
     middle = x1[...].astype(BF16)
-    before, after = shifted(middle)
-    x1s[pl.ds(0, per), :] = before
+    store_shifted(x1s, 0, 2 * per, per, middle)
     x1s[pl.ds(per, per), :] = middle
-    x1s[pl.ds(2 * per, per), :] = after
     tiles = cols // TILE
 
     def layer1(t, carry):
         start = pl.multiple_of(t * TILE, TILE)
-        value = silu(dot(w1[...], x1s[:, pl.ds(start, TILE)]) + bias1).astype(BF16)
+        value = silu_of_half(dot(w1[...], x1s[:, pl.ds(start, TILE)])).astype(BF16)
         for r in range(rows):
             x2[pl.ds((r * 3 + 1) * k2, k2), pl.ds(start, TILE)] = value[r * k2 : (r + 1) * k2]
         return carry
@@ -242,27 +255,31 @@
         for r in range(rows):
             base = r * 3 * k2 + n * ch
             values = x2[pl.ds(pl.multiple_of(base + k2, ch), ch), :]
-            before, after = shifted(values)
-            x2[pl.ds(pl.multiple_of(base, ch), ch), :] = before
-            x2[pl.ds(pl.multiple_of(base + 2 * k2, ch), ch), :] = after
+            store_shifted(
+                x2, pl.multiple_of(base, ch), pl.multiple_of(base + 2 * k2, ch), ch, values
+            )
         return carry
 
     lax.fori_loop(0, out1, shift2, 0)
+
+    ramps = 2 * narrow // tiles
 
     def layer2(t, carry):
         start = pl.multiple_of(t * TILE, TILE)
         for r in range(rows):
-            value = silu(dot(w2[...], x2[pl.ds(r * 3 * k2, 3 * k2), pl.ds(start, TILE)]) + bias2)
-            x3[pl.ds(r * out2 * ch, out2 * ch), :] = value.astype(BF16)
-        taps[:, pl.ds(start, TILE)] = dot(w3[...], x3[...])[0 : 3 * ar]
+            value = dot(w2[...], x2[pl.ds(r * 3 * k2, 3 * k2), pl.ds(start, TILE)]) + bias2
+            x3[pl.ds(r * out2 * ch, out2 * ch), pl.ds(start, TILE)] = silu_of_half(value).astype(BF16)
+        for n in range(ramps):
+            ramp_block(t * ramps + n)
         return carry
 
     lax.fori_loop(0, tiles, layer2, 0)
 
+    taps = dot(w3[...], x3[...])
     column = iota((ar, cols), 1)
-    before = jnp.where(column == 0, 0.0, pltpu.roll(taps[0:ar, :], 1, 1))
-    after = jnp.where(column == cols - 1, 0.0, pltpu.roll(taps[2 * ar : 3 * ar, :], cols - 1, 1))
-    update = before + taps[ar : 2 * ar, :] + after
+    before = jnp.where(column == 0, 0.0, pltpu.roll(taps[0:ar], 1, 1))
+    after = jnp.where(column == cols - 1, 0.0, pltpu.roll(taps[2 * ar : 3 * ar], cols - 1, 1))
+    update = before + taps[ar : 2 * ar] + after
     own = x1[pl.ds(3 * rows, ar), :]
     new_dual = (own + update).astype(BF16).astype(F32)
     for a in range(angs):
@@ -286,6 +303,19 @@
     centre = (cols - 1) / 2.0
     mags = by_row(mag, (ar, 128), angs)
     shifts = by_row(shift, (ar, 128), angs)
+    halves = cols // n_ang // 128
+    size = halves * ar
+
+    def block_copy(source, target, ang, row):
+        return pltpu.make_async_remote_copy(
+            src_ref=sent.at[ang],
+            dst_ref=got.at[source],
+            send_sem=send_sem.at[target],
+            recv_sem=recv_sem.at[source],
+            device_id=(ang, row),
+            device_id_type=MESH,
+        )
+
     projected = []
     for n in range(cols // 128):
         edges = [
@@ -308,28 +338,19 @@
                 value = jnp.where(index >> 7 == k, taken, value)
             ends.append(value)
         projected.append((1.0 - weight) * ends[0] + weight * ends[1])
-
-    halves = cols // n_ang // 128
-    size = halves * ar
-    for p in range(n_ang):
-        sent[p] = jnp.concatenate(projected[p * halves : (p + 1) * halves], axis=0).astype(BF16)
-
-    def block_copy(source, target, ang, row):
-        return pltpu.make_async_remote_copy(
-            src_ref=sent.at[ang],
-            dst_ref=got.at[source],
-            send_sem=send_sem.at[target],
-            recv_sem=recv_sem.at[source],
-            device_id=(ang, row),
-            device_id_type=MESH,
-        )
-
-    def block_start(step, carry):
-        target, ang, row = place_of(step)
-        block_copy(me, target, ang, row).start()
-        return carry
-
-    lax.fori_loop(1, total, block_start, 0)
+        if len(projected) == halves:
+            p = n // halves
+            sent[p] = jnp.concatenate(projected, axis=0).astype(BF16)
+            projected = []
+            for step in range(1, n_row):
+                row = lax.rem(my_row + step, n_row)
+                block_copy(me, p * n_row + row, p, row).start()
+
+            @pl.when(my_ang != p)
+            def _():
+                block_copy(me, p * n_row + my_row, p, my_row).start()
+
+
     got[me] = sent[my_ang]
 
     def frac_wait(step, carry):
@@ -415,12 +436,12 @@
             pltpu.VMEM((64, cols), F32),
             pltpu.VMEM((3 * 64, cols), BF16),
             pltpu.VMEM((rows * 3 * out1 * ch, cols), BF16),
-            pltpu.VMEM((rows * out2 * ch, TILE), BF16),
-            pltpu.VMEM((3 * ar, cols), F32),
+            pltpu.VMEM((rows * out2 * ch, cols), BF16),
+            pltpu.VMEM((32, ch), F32),
             pltpu.VMEM((rows * out1 * ch, 3 * 64), BF16),
             pltpu.VMEM((out2 * ch, 3 * out1 * ch), BF16),
             pltpu.VMEM((4 * ar, rows * out2 * ch), BF16),
-            pltpu.VMEM((128, (2 * narrow - 1) * 128), BF16),
+            pltpu.VMEM((128, 2 * narrow * 128), BF16),
             pltpu.VMEM((8, 128), F32),
             pltpu.VMEM((n_ang, 8, 128), F32),
             pltpu.VMEM((n_ang, size, 128), BF16),

time: 29.5 us -> 26.5 us (0.90)
  Pallas kernels: 26.7 us -> 23.6 us
    pallas_call x1, Pallas kernels: 26.7 us -> 23.6 us  [per_device(): pl.pallas_call(functools.partial(kernel, n_ang, n_row), out_shape=(jax.Sh...]
where the time goes in v3:
time: 26.5 us; the launch traced here: 26.3 us
  Pallas kernels  23.6 us (89%)
  local copies, waits for them, and re-layouts  2.01 us (8%)
  between operations  0.65 us (2%)
    pallas_call x1, Pallas kernels, per_device(): pl.pallas_call(functools.partial(kernel, n_ang, n_row), out_shape=(jax.Sh...  23.6 us
    unnamed x4, local copies, waits for them, and re-layouts  2.01 us

profile of v3, /device:TPU:0, one launch (start us, length us, event | category | flops | bytes accessed | tf_op | source)
XLA Modules:
  0.0 26.3 jit_solution(4939931858736072263)
XLA Ops:
  0.6 23.6 %shard_map.140 = (bf16[4,2,2048]{2,1,0:T(2,128)(2,1)}, f32[16,256]{1,0:T(8,128)}) custom-call(bf16[4,2,2048]{2,1,0:T(2,128)(2,1)} %refs_0_.1, bf16[4,2,2048]{2,1,0:T(2,128)(2,1)} %refs_1_.1, bf16[4,2,2048]{2,1,0:T(2,128)(2,1)} %refs_2_.1, bf16[3,3,3,32]{3,2,1,0:T(4,128)(2,1)} %bitcast.4, f32[1,32]{1,0:T(1,128)} %bitcast.6, bf16[3,3,32,32]{3,2,1,0:T(8,128)(2,1)} %refs_5_.1, ...), custom_call_target="tpu_custom_call" | custom-call | flops 1000000000 | bytes 1000000 | tf_op jit(solution)/shard_map/pallas_call | solution.py:424
  24.3 0.0 copy-start
  24.3 1.4 %copy.17 = bf16[4,2,2048]{2,1,0:T(2,128)(2,1)} copy(bf16[4,2,2048]{2,1,0:T(2,128)(2,1)} %get-tuple-element.4) | data formatting | bytes 65536
  25.7 0.0 copy-done
  25.7 0.6 %copy.18 = f32[16,256]{1,0:T(8,128)} copy(f32[16,256]{1,0:T(8,128)S(1)} %copy-done) | data formatting | bytes 32768
Async XLA Ops:
  24.3 1.4 %copy-start = (f32[16,256]{1,0:T(8,128)S(1)}, f32[16,256]{1,0:T(8,128)}, u32[]{:S(2)}) copy-start(f32[16,256]{1,0:T(8,128)} %get-tuple-element.5) | copy-start | bytes 49156

commit v4 on v3

--- a/solution.py
+++ b/solution.py
@@ -83,8 +83,6 @@
         pltpu.make_async_copy(source, goal, local_sem.at[n])
         for n, (source, goal) in enumerate(zip(sources, locals_))
     ]
-    for load in loads:
-        load.start()
     angs, rows, cols = dual.shape
     ch = mw.shape[2]
     total = n_ang * n_row
@@ -107,6 +105,8 @@
         return carry
 
     lax.fori_loop(1, total, greet, 0)
+    for load in loads:
+        load.start()
 
     narrow = cols // 128
 
@@ -245,22 +245,29 @@
     def layer1(t, carry):
         start = pl.multiple_of(t * TILE, TILE)
         value = silu_of_half(dot(w1[...], x1s[:, pl.ds(start, TILE)])).astype(BF16)
+        before = pltpu.roll(value, 1, 1)
+        after = pltpu.roll(value, TILE - 1, 1)
         for r in range(rows):
-            x2[pl.ds((r * 3 + 1) * k2, k2), pl.ds(start, TILE)] = value[r * k2 : (r + 1) * k2]
+            for j, whole in enumerate((before, value, after)):
+                x2[pl.ds((r * 3 + j) * k2, k2), pl.ds(start, TILE)] = whole[r * k2 : (r + 1) * k2]
         return carry
 
     lax.fori_loop(0, tiles, layer1, 0)
 
-    def shift2(n, carry):
-        for r in range(rows):
-            base = r * 3 * k2 + n * ch
-            values = x2[pl.ds(pl.multiple_of(base + k2, ch), ch), :]
-            store_shifted(
-                x2, pl.multiple_of(base, ch), pl.multiple_of(base + 2 * k2, ch), ch, values
-            )
-        return carry
-
-    lax.fori_loop(0, out1, shift2, 0)
+    edge = iota((k2, 128), 1)
+    zero = jnp.zeros((k2, 128), BF16)
+    for r in range(rows):
+        low, mid, high = [pl.ds((r * 3 + j) * k2, k2) for j in range(3)]
+        for t in range(tiles):
+            first, last = pl.ds(t * TILE, 128), pl.ds((t + 1) * TILE - 128, 128)
+            beyond = zero
+            if t > 0:
+                beyond = pltpu.roll(x2[mid, pl.ds(t * TILE - 128, 128)], 1, 1)
+            x2[low, first] = jnp.where(edge == 0, beyond, x2[low, first])
+            beyond = zero
+            if t < tiles - 1:
+                beyond = pltpu.roll(x2[mid, pl.ds((t + 1) * TILE, 128)], 127, 1)
+            x2[high, last] = jnp.where(edge == 127, beyond, x2[high, last])
 
     ramps = 2 * narrow // tiles
 
@@ -424,8 +431,8 @@
     return pl.pallas_call(
         functools.partial(kernel, n_ang, n_row),
         out_shape=(
-            jax.ShapeDtypeStruct(dual_field.shape, BF16),
-            jax.ShapeDtypeStruct((slots * SLAB_Z, width), F32),
+            pltpu.VMEM(dual_field.shape, BF16),
+            pltpu.VMEM((slots * SLAB_Z, width), F32),
         ),
         in_specs=[pl.BlockSpec(memory_space=pltpu.HBM)] * 13,
         out_specs=(vmem, vmem),

time: 26.5 us -> 24.3 us (0.917)
  Pallas kernels: 23.6 us -> 22.2 us
  local copies, waits for them, and re-layouts: 2.01 us -> 1.22 us
    pallas_call x1, Pallas kernels: 23.6 us -> 22.2 us  [per_device(): pl.pallas_call(functools.partial(kernel, n_ang, n_row), out_shape=(pltpu....]
    unnamed x4 -> x2, local copies, waits for them, and re-layouts: 2.01 us -> 1.22 us
where the time goes in v4:
time: 24.3 us; the launch traced here: 24.1 us
  Pallas kernels  22.2 us (91%)
  local copies, waits for them, and re-layouts  1.22 us (5%)
  between operations  0.64 us (3%)
    pallas_call x1, Pallas kernels, per_device(): pl.pallas_call(functools.partial(kernel, n_ang, n_row), out_shape=(pltpu....  22.2 us
    unnamed x2, local copies, waits for them, and re-layouts  1.22 us

profile of v4, /device:TPU:0, one launch (start us, length us, event | category | flops | bytes accessed | tf_op | source)
XLA Modules:
  0.0 24.1 jit_solution(16203488830407955468)
XLA Ops:
  0.6 22.2 %shard_map.140 = (bf16[4,2,2048]{2,1,0:T(2,128)(2,1)S(1)}, f32[16,256]{1,0:T(8,128)S(1)}) custom-call(bf16[4,2,2048]{2,1,0:T(2,128)(2,1)} %refs_0_.1, bf16[4,2,2048]{2,1,0:T(2,128)(2,1)} %refs_1_.1, bf16[4,2,2048]{2,1,0:T(2,128)(2,1)} %refs_2_.1, bf16[3,3,3,32]{3,2,1,0:T(4,128)(2,1)} %bitcast.4, f32[1,32]{1,0:T(1,128)} %bitcast.6, ...), custom_call_target="tpu_custom_call" | custom-call | flops 1000000000 | bytes 1000000 | tf_op jit(solution)/shard_map/pallas_call | solution.py:431
  22.9 0.6 %copy.17 = bf16[4,2,2048]{2,1,0:T(2,128)(2,1)} copy(bf16[4,2,2048]{2,1,0:T(2,128)(2,1)S(1)} %get-tuple-element.2) | data formatting | bytes 65536
  23.5 0.6 %copy.18 = f32[16,256]{1,0:T(8,128)} copy(f32[16,256]{1,0:T(8,128)S(1)} %get-tuple-element.3) | data formatting | bytes 32768

commit v5 on v4

--- a/solution.py
+++ b/solution.py
@@ -117,49 +117,8 @@
         value = jnp.where(odd, -1.0 / (math.pi * math.pi * distance * distance), 0.0)
         ramp[:, pl.ds(pl.multiple_of(b * 128, 128), 128)] = jnp.where(away == 0, 0.25, value).astype(BF16)
 
-    pl.semaphore_wait(barrier, total - 1)
-
-    left = lax.rem(my_ang + n_ang - 1, n_ang)
-    right = lax.rem(my_ang + 1, n_ang)
-    halo_copies = []
-    for c, ref in enumerate(sources[:3]):
-        for side, (peer, first) in enumerate(((right, angs - 3), (left, 0))):
-            copy = pltpu.make_async_remote_copy(
-                src_ref=ref.at[pl.ds(first, 3)],
-                dst_ref=halo.at[side, c],
-                send_sem=halo_send.at[side, c],
-                recv_sem=halo_recv.at[side, c],
-                device_id=(peer, my_row),
-                device_id_type=MESH,
-            )
-            copy.start()
-            halo_copies.append(copy)
-
     for load in loads:
         load.wait()
-    lane = iota((8, 128), 1)
-    mine = jnp.full((8, 128), frac[0], F32)
-    for a in range(1, angs):
-        mine = jnp.where((lane & (ar - 1)) // rows == a, frac[a], mine)
-    frac_own[...] = mine
-    frac_all[my_ang] = mine
-
-    def frac_copy(source, target):
-        return pltpu.make_async_remote_copy(
-            src_ref=frac_own,
-            dst_ref=frac_all.at[source],
-            send_sem=frac_send.at[target],
-            recv_sem=frac_recv.at[source],
-            device_id=(target, my_row),
-            device_id_type=MESH,
-        )
-
-    def frac_start(step, carry):
-        frac_copy(my_ang, lax.rem(my_ang + step, n_ang)).start()
-        return carry
-
-    lax.fori_loop(1, n_ang, frac_start, 0)
-
     k1 = 3 * per
     tap1, rest1 = split(iota((ch, k1), 1), per, 3)
     chan1, rest1 = split(rest1, wide * rows, 4)
@@ -192,18 +151,6 @@
                 block = jnp.where((ang1 == a + i) & (row1 == r), joined1[i], block)
             w1[pl.ds((r * out1 + a) * ch, ch), :] = block.astype(BF16)
 
-    k2 = out1 * ch
-    pick2 = jnp.where((iota((ch, k2), 1) & (ch - 1)) == iota((ch, k2), 0), 0.5, 0.0).astype(BF16)
-    ang2, _ = split(iota((ch, k2), 1), ch, out1)
-    all2 = dot(mw[...].reshape(9 * ch, ch), pick2)
-    for j in range(3):
-        tiles2 = [all2[(i * 3 + j) * ch : (i * 3 + j + 1) * ch] for i in range(3)]
-        for a in range(out2):
-            block = jnp.zeros((ch, k2), F32)
-            for i in range(3):
-                block = jnp.where(ang2 == a + i, tiles2[i], block)
-            w2[pl.ds(a * ch, ch), pl.ds(j * k2, k2)] = block.astype(BF16)
-
     k3 = rows * out2 * ch
     pick3 = jnp.where((iota((ch, k3), 1) & (ch - 1)) == iota((ch, k3), 0), 1.0, 0.0).astype(BF16)
     row3, rest3 = split(iota((ar, k3), 1), out2 * ch, rows)
@@ -224,6 +171,59 @@
     blocks3.append(jnp.zeros((ar, k3), F32))
     w3[...] = jnp.concatenate(blocks3, axis=0).astype(BF16)
 
+    pl.semaphore_wait(barrier, total - 1)
+
+    left = lax.rem(my_ang + n_ang - 1, n_ang)
+    right = lax.rem(my_ang + 1, n_ang)
+    halo_copies = []
+    for c, ref in enumerate(sources[:3]):
+        for side, (peer, first) in enumerate(((right, angs - 3), (left, 0))):
+            copy = pltpu.make_async_remote_copy(
+                src_ref=ref.at[pl.ds(first, 3)],
+                dst_ref=halo.at[side, c],
+                send_sem=halo_send.at[side, c],
+                recv_sem=halo_recv.at[side, c],
+                device_id=(peer, my_row),
+                device_id_type=MESH,
+            )
+            copy.start()
+            halo_copies.append(copy)
+
+    lane = iota((8, 128), 1)
+    mine = jnp.full((8, 128), frac[0], F32)
+    for a in range(1, angs):
+        mine = jnp.where((lane & (ar - 1)) // rows == a, frac[a], mine)
+    frac_own[...] = mine
+    frac_all[my_ang] = mine
+
+    def frac_copy(source, target):
+        return pltpu.make_async_remote_copy(
+            src_ref=frac_own,
+            dst_ref=frac_all.at[source],
+            send_sem=frac_send.at[target],
+            recv_sem=frac_recv.at[source],
+            device_id=(target, my_row),
+            device_id_type=MESH,
+        )
+
+    def frac_start(step, carry):
+        frac_copy(my_ang, lax.rem(my_ang + step, n_ang)).start()
+        return carry
+
+    lax.fori_loop(1, n_ang, frac_start, 0)
+
+    k2 = out1 * ch
+    pick2 = jnp.where((iota((ch, k2), 1) & (ch - 1)) == iota((ch, k2), 0), 0.5, 0.0).astype(BF16)
+    ang2, _ = split(iota((ch, k2), 1), ch, out1)
+    all2 = dot(mw[...].reshape(9 * ch, ch), pick2)
+    for j in range(3):
+        tiles2 = [all2[(i * 3 + j) * ch : (i * 3 + j + 1) * ch] for i in range(3)]
+        for a in range(out2):
+            block = jnp.zeros((ch, k2), F32)
+            for i in range(3):
+                block = jnp.where(ang2 == a + i, tiles2[i], block)
+            w2[pl.ds(a * ch, ch), pl.ds(j * k2, k2)] = block.astype(BF16)
+
     bias2 = jnp.concatenate([as_column(mb[...]) * 0.5] * out2, axis=0)
 
     used = 3 * wide * rows
@@ -313,12 +313,12 @@
     halves = cols // n_ang // 128
     size = halves * ar
 
-    def block_copy(source, target, ang, row):
+    def block_copy(source, ang, row):
         return pltpu.make_async_remote_copy(
             src_ref=sent.at[ang],
             dst_ref=got.at[source],
-            send_sem=send_sem.at[target],
-            recv_sem=recv_sem.at[source],
+            send_sem=send_sem,
+            recv_sem=recv_sem,
             device_id=(ang, row),
             device_id_type=MESH,
         )
@@ -351,11 +351,11 @@
             projected = []
             for step in range(1, n_row):
                 row = lax.rem(my_row + step, n_row)
-                block_copy(me, p * n_row + row, p, row).start()
+                block_copy(me, p, row).start()
 
             @pl.when(my_ang != p)
             def _():
-                block_copy(me, p * n_row + my_row, p, my_row).start()
+                block_copy(me, p, my_row).start()
 
 
     got[me] = sent[my_ang]
@@ -395,17 +395,14 @@
             parts.append(part)
     stacked = jnp.concatenate(parts, axis=0)
 
-    def block_wait(step, carry):
-        target, ang, row = place_of(step)
-        block_copy(target, target, ang, row).wait()
-        return carry
-
-    lax.fori_loop(1, total, block_wait, 0)
+    others = got.at[pl.ds(0, total - 1)]
+    pltpu.make_async_copy(others, others, recv_sem).wait()
 
     sums = dot(stacked, got[...].reshape(depth, 128))
     for h in range(halves):
         three = [sums[(h * 3 + s) * zs : (h * 3 + s + 1) * zs] for s in range(3)]
         vol_out[:, pl.ds(h * 128, 128)] = (three[2] + three[1] + three[0]) / math.sqrt(n_ang * angs)
+    pltpu.make_async_copy(others, others, send_sem).wait()
 
 
 def per_device(
@@ -428,7 +425,7 @@
     slots = slab_order.shape[0] // n_row
     vmem = pl.BlockSpec(memory_space=pltpu.VMEM)
     dma = pltpu.SemaphoreType.DMA
-    return pl.pallas_call(
+    results = pl.pallas_call(
         functools.partial(kernel, n_ang, n_row),
         out_shape=(
             pltpu.VMEM(dual_field.shape, BF16),
@@ -457,8 +454,8 @@
             dma((2, 3)),
             dma((n_ang,)),
             dma((n_ang,)),
-            dma((total,)),
-            dma((total,)),
+            dma(()),
+            dma(()),
             dma((13,)),
         ],
         compiler_params=pltpu.CompilerParams(
@@ -466,6 +463,23 @@
         ),
         cost_estimate=pl.CostEstimate(flops=10**9, bytes_accessed=10**6, transcendentals=0),
     )(*operands)
+    hbm = pl.BlockSpec(memory_space=pltpu.HBM)
+    return pl.pallas_call(
+        write_out,
+        out_shape=tuple(jax.ShapeDtypeStruct(x.shape, x.dtype) for x in results),
+        in_specs=[vmem, vmem],
+        out_specs=(hbm, hbm),
+        scratch_shapes=[dma((2,))],
+    )(*results)
+
+
+def write_out(nd_in, vol_in, nd_out, vol_out, sems):
+    first = pltpu.make_async_copy(nd_in, nd_out, sems.at[0])
+    second = pltpu.make_async_copy(vol_in, vol_out, sems.at[1])
+    first.start()
+    second.start()
+    first.wait()
+    second.wait()
 
 
 def solution(mesh):

time: 24.3 us -> 25.2 us (1.037)
  Pallas kernels: 22.2 us -> 23.1 us
    pallas_call x0 -> x1, Pallas kernels: none -> 1.39 us  [per_device(): pl.pallas_call(write_out, out_shape=tuple((jax.ShapeDtypeStruct(x.shape,...]
    pallas_call x1, Pallas kernels: 22.2 us -> 21.7 us  [per_device(): pl.pallas_call(functools.partial(kernel, n_ang, n_row), out_shape=(pltpu....]
    unnamed x2 -> x4, local copies, waits for them, and re-layouts: 1.22 us -> 1.2 us
where the time goes in v5:
time: 25.2 us; the launch traced here: 24.9 us
  Pallas kernels  23.1 us (92%)
  local copies, waits for them, and re-layouts  1.2 us (5%)
  between operations  0.65 us (3%)
    pallas_call x1, Pallas kernels, per_device(): pl.pallas_call(functools.partial(kernel, n_ang, n_row), out_shape=(pltpu....  21.7 us
    pallas_call x1, Pallas kernels, per_device(): pl.pallas_call(write_out, out_shape=tuple((jax.ShapeDtypeStruct(x.shape,...  1.39 us
    unnamed x4, local copies, waits for them, and re-layouts  1.2 us

profile of v5, /device:TPU:0, one launch (start us, length us, event | category | flops | bytes accessed | tf_op | source)
XLA Modules:
  0.0 24.9 jit_solution(9389662893367960597)
XLA Ops:
  0.6 21.7 %shard_map.140 = (bf16[4,2,2048]{2,1,0:T(2,128)(2,1)S(1)}, f32[16,256]{1,0:T(8,128)S(1)}) custom-call(bf16[4,2,2048]{2,1,0:T(2,128)(2,1)} %refs_0_.1, bf16[4,2,2048]{2,1,0:T(2,128)(2,1)} %refs_1_.1, bf16[4,2,2048]{2,1,0:T(2,128)(2,1)} %refs_2_.1, bf16[3,3,3,32]{3,2,1,0:T(4,128)(2,1)} %bitcast.4, f32[1,32]{1,0:T(1,128)} %bitcast.6, ...), custom_call_target="tpu_custom_call" | custom-call | flops 1000000000 | bytes 1000000 | tf_op jit(solution)/shard_map/pallas_call | solution.py:428
  22.3 0.0 copy-start
  22.4 0.6 %copy-done = bf16[4,2,2048]{2,1,0:T(2,128)(2,1)} copy-done((bf16[4,2,2048]{2,1,0:T(2,128)(2,1)}, bf16[4,2,2048]{2,1,0:T(2,128)(2,1)S(1)}, u32[]{:S(2)}) %copy-start) | copy-done | bytes 32792
  23.0 0.0 copy-start.1
  23.0 0.6 %copy-done.1 = f32[16,256]{1,0:T(8,128)} copy-done((f32[16,256]{1,0:T(8,128)}, f32[16,256]{1,0:T(8,128)S(1)}, u32[]{:S(2)}) %copy-start.1) | copy-done | bytes 16408
  23.6 1.4 %shard_map.141 = (bf16[4,2,2048]{2,1,0:T(2,128)(2,1)}, f32[16,256]{1,0:T(8,128)}) custom-call(bf16[4,2,2048]{2,1,0:T(2,128)(2,1)} %copy-done, f32[16,256]{1,0:T(8,128)} %copy-done.1), custom_call_target="tpu_custom_call" | custom-call | tf_op jit(solution)/shard_map/pallas_call | solution.py:467
Async XLA Ops:
  22.3 0.6 %copy-start = (bf16[4,2,2048]{2,1,0:T(2,128)(2,1)}, bf16[4,2,2048]{2,1,0:T(2,128)(2,1)S(1)}, u32[]{:S(2)}) copy-start(bf16[4,2,2048]{2,1,0:T(2,128)(2,1)S(1)} %get-tuple-element.4.nd_in) | copy-start | bytes 98308
  23.0 0.6 %copy-start.1 = (f32[16,256]{1,0:T(8,128)}, f32[16,256]{1,0:T(8,128)S(1)}, u32[]{:S(2)}) copy-start(f32[16,256]{1,0:T(8,128)S(1)} %get-tuple-element.5.vol_in) | copy-start | bytes 49156

commit v6 on v5

--- a/solution.py
+++ b/solution.py
@@ -425,7 +425,7 @@
     slots = slab_order.shape[0] // n_row
     vmem = pl.BlockSpec(memory_space=pltpu.VMEM)
     dma = pltpu.SemaphoreType.DMA
-    results = pl.pallas_call(
+    return pl.pallas_call(
         functools.partial(kernel, n_ang, n_row),
         out_shape=(
             pltpu.VMEM(dual_field.shape, BF16),
@@ -463,23 +463,6 @@
         ),
         cost_estimate=pl.CostEstimate(flops=10**9, bytes_accessed=10**6, transcendentals=0),
     )(*operands)
-    hbm = pl.BlockSpec(memory_space=pltpu.HBM)
-    return pl.pallas_call(
-        write_out,
-        out_shape=tuple(jax.ShapeDtypeStruct(x.shape, x.dtype) for x in results),
-        in_specs=[vmem, vmem],
-        out_specs=(hbm, hbm),
-        scratch_shapes=[dma((2,))],
-    )(*results)
-
-
-def write_out(nd_in, vol_in, nd_out, vol_out, sems):
-    first = pltpu.make_async_copy(nd_in, nd_out, sems.at[0])
-    second = pltpu.make_async_copy(vol_in, vol_out, sems.at[1])
-    first.start()
-    second.start()
-    first.wait()
-    second.wait()
 
 
 def solution(mesh):

time: 25.2 us -> 23.7 us (0.940)
  Pallas kernels: 23.1 us -> 21.7 us
    pallas_call x1 -> x0, Pallas kernels: 1.39 us -> none  [per_device(): pl.pallas_call(write_out, out_shape=tuple((jax.ShapeDtypeStruct(x.shape,...]
    unnamed x4 -> x2, local copies, waits for them, and re-layouts: 1.2 us -> 1.22 us
where the time goes in v6:
time: 23.7 us; the launch traced here: 23.6 us
  Pallas kernels  21.7 us (92%)
  local copies, waits for them, and re-layouts  1.22 us (5%)
  between operations  0.64 us (3%)
    pallas_call x1, Pallas kernels, per_device(): pl.pallas_call(functools.partial(kernel, n_ang, n_row), out_shape=(pltpu....  21.7 us
    unnamed x2, local copies, waits for them, and re-layouts  1.22 us

profile of v6, /device:TPU:0, one launch (start us, length us, event | category | flops | bytes accessed | tf_op | source)
XLA Modules:
  0.0 23.6 jit_solution(11292014000095094799)
XLA Ops:
  0.6 21.7 %shard_map.140 = (bf16[4,2,2048]{2,1,0:T(2,128)(2,1)S(1)}, f32[16,256]{1,0:T(8,128)S(1)}) custom-call(bf16[4,2,2048]{2,1,0:T(2,128)(2,1)} %refs_0_.1, bf16[4,2,2048]{2,1,0:T(2,128)(2,1)} %refs_1_.1, bf16[4,2,2048]{2,1,0:T(2,128)(2,1)} %refs_2_.1, bf16[3,3,3,32]{3,2,1,0:T(4,128)(2,1)} %bitcast.4, f32[1,32]{1,0:T(1,128)} %bitcast.6, ...), custom_call_target="tpu_custom_call" | custom-call | flops 1000000000 | bytes 1000000 | tf_op jit(solution)/shard_map/pallas_call | solution.py:428
  22.3 0.6 %copy.17 = bf16[4,2,2048]{2,1,0:T(2,128)(2,1)} copy(bf16[4,2,2048]{2,1,0:T(2,128)(2,1)S(1)} %get-tuple-element.2) | data formatting | bytes 65536
  23.0 0.6 %copy.18 = f32[16,256]{1,0:T(8,128)} copy(f32[16,256]{1,0:T(8,128)S(1)} %get-tuple-element.3) | data formatting | bytes 32768

commit v7 on v6

--- a/solution.py
+++ b/solution.py
@@ -171,6 +171,11 @@
     blocks3.append(jnp.zeros((ar, k3), F32))
     w3[...] = jnp.concatenate(blocks3, axis=0).astype(BF16)
 
+    used = 3 * wide * rows
+    x1[pl.ds(per - 8, 8), :] = jnp.where(iota((8, cols), 0) + per - 8 < used + 3, 1.0, 0.0)
+    for c, ref in enumerate((dual, forward, sino)):
+        for a in range(angs):
+            x1[pl.ds((c * wide + 3 + a) * rows, rows), :] = ref[a].astype(F32)
     pl.semaphore_wait(barrier, total - 1)
 
     left = lax.rem(my_ang + n_ang - 1, n_ang)
@@ -226,13 +231,8 @@
 
     bias2 = jnp.concatenate([as_column(mb[...]) * 0.5] * out2, axis=0)
 
-    used = 3 * wide * rows
-    x1[pl.ds(per - 8, 8), :] = jnp.where(iota((8, cols), 0) + per - 8 < used + 3, 1.0, 0.0)
-    for c, ref in enumerate((dual, forward, sino)):
-        for a in range(angs):
-            x1[pl.ds((c * wide + 3 + a) * rows, rows), :] = ref[a].astype(F32)
     for copy in halo_copies:
-        copy.wait()
+        copy.wait_recv()
     for c in range(3):
         for a in range(3):
             x1[pl.ds((c * wide + a) * rows, rows), :] = halo[0, c, a].astype(F32)
@@ -403,6 +403,8 @@
         three = [sums[(h * 3 + s) * zs : (h * 3 + s + 1) * zs] for s in range(3)]
         vol_out[:, pl.ds(h * 128, 128)] = (three[2] + three[1] + three[0]) / math.sqrt(n_ang * angs)
     pltpu.make_async_copy(others, others, send_sem).wait()
+    for copy in halo_copies:
+        copy.wait_send()
 
 
 def per_device(

time: 23.7 us -> 23.7 us (level)
  no operation moved by 1% of the time
where the time goes in v7:
time: 23.7 us; the launch traced here: 23.5 us
  Pallas kernels  21.7 us (92%)
  local copies, waits for them, and re-layouts  1.22 us (5%)
  between operations  0.64 us (3%)
    pallas_call x1, Pallas kernels, per_device(): pl.pallas_call(functools.partial(kernel, n_ang, n_row), out_shape=(pltpu....  21.7 us
    unnamed x2, local copies, waits for them, and re-layouts  1.22 us

profile of v7, /device:TPU:0, one launch (start us, length us, event | category | flops | bytes accessed | tf_op | source)
XLA Modules:
  0.0 23.5 jit_solution(4206096958338398730)
XLA Ops:
  0.6 21.7 %shard_map.140 = (bf16[4,2,2048]{2,1,0:T(2,128)(2,1)S(1)}, f32[16,256]{1,0:T(8,128)S(1)}) custom-call(bf16[4,2,2048]{2,1,0:T(2,128)(2,1)} %refs_0_.1, bf16[4,2,2048]{2,1,0:T(2,128)(2,1)} %refs_1_.1, bf16[4,2,2048]{2,1,0:T(2,128)(2,1)} %refs_2_.1, bf16[3,3,3,32]{3,2,1,0:T(4,128)(2,1)} %bitcast.4, f32[1,32]{1,0:T(1,128)} %bitcast.6, ...), custom_call_target="tpu_custom_call" | custom-call | flops 1000000000 | bytes 1000000 | tf_op jit(solution)/shard_map/pallas_call | solution.py:430
  22.3 0.6 %copy.17 = bf16[4,2,2048]{2,1,0:T(2,128)(2,1)} copy(bf16[4,2,2048]{2,1,0:T(2,128)(2,1)S(1)} %get-tuple-element.2) | data formatting | bytes 65536
  22.9 0.6 %copy.18 = f32[16,256]{1,0:T(8,128)} copy(f32[16,256]{1,0:T(8,128)S(1)} %get-tuple-element.3) | data formatting | bytes 32768
